TPU v7x, 1024 devices: a whole 4x8x16 slice. The times are simulated.
1024 devices in a mesh: dp: 32 (over y, x), expert: 32 (over z, core).
Axes of the slice: x: 4, y: 8, z: 16, core: 2. Of those that a mesh axis runs over, the one named last changes fastest.
Arguments:
- latent: bfloat16 [131072, 512], P(('dp', 'expert')), may hold values from -6 to 6
- up_proj: bfloat16 [512, 4096], P(None, 'expert'), may hold values from -0.25 to 0.25
- expert_in: bfloat16 [32, 512, 4096], P('expert'), may hold values from -0.25 to 0.25
- expert_out: bfloat16 [32, 2048, 512], P('expert'), may hold values from -0.125 to 0.125
- routes: int32 [131072, 8], P(('dp', 'expert')), may hold values from 0 to 127, all different within a row; in each aligned block of 128 rows (0 to 127, 128 to 255, ...) at most 13 rows name the same one
- gates: bfloat16 [131072, 8], P(('dp', 'expert')), may hold values from 0.099609375 to 1
- cotangent: bfloat16 [131072, 4096], P('dp', 'expert'), may hold values from -6 to 6
Outputs:
- mixed: bfloat16 [131072, 4096], P('dp', 'expert')
- grad_up: float32 [512, 4096], P(None, 'expert')
Inputs may be any that keep to these rules, and one draw needn't show every extreme that they name: `routes`: in each aligned block of 128 rows (the tokens of one device) no expert is named more than 13 times.
All inputs are finite; a program needn't handle non-finite values.
Results may differ from a plain program's by a relative error of at most 0.0064.
Values may be sent and summed in bfloat16 or wider, within the bound.
No kernel may reach another device: no remote copies, remote signals or barrier semaphores. Data moves between devices by JAX's collectives and lax.ppermute only.
A program may use at most 32 MiB of HBM per device.

v0:
```python
import jax
import jax.numpy as jnp
from jax import lax
from jax.sharding import PartitionSpec as P

TOP = 8
CAP = 13


def body(latent, up_proj, expert_in, expert_out, routes, gates, cotangent):
    n_expert = lax.axis_size("expert")
    tok_dev = routes.shape[0]
    width = latent.shape[1]
    hidden = expert_out.shape[1]
    flat = routes.reshape(-1)
    inside = flat < n_expert
    onehot = (flat[:, None] == jnp.arange(n_expert, dtype=jnp.int32)[None, :]).astype(jnp.int32)
    before = jnp.cumsum(onehot, axis=0) - onehot
    slot = jnp.sum(before * onehot, axis=1)
    target = jnp.where(inside, flat * CAP + slot, -1)
    place = (jnp.arange(n_expert * CAP, dtype=jnp.int32)[:, None] == target[None, :]).astype(
        jnp.float32
    )
    owner = (
        jnp.arange(flat.shape[0], dtype=jnp.int32)[:, None] // TOP
        == jnp.arange(tok_dev, dtype=jnp.int32)[None, :]
    ).astype(jnp.float32)
    dispatch = jnp.dot(place, owner, precision=lax.Precision.HIGHEST).astype(jnp.bfloat16)
    weighted = owner * gates.reshape(-1).astype(jnp.float32)[:, None]
    weighting = jnp.dot(weighted.T, place.T, precision=lax.Precision.HIGHEST).astype(jnp.bfloat16)
    outgoing = jnp.dot(dispatch, latent, preferred_element_type=jnp.float32).astype(jnp.bfloat16)
    outgoing = outgoing.reshape(n_expert, CAP, width)
    arrived = lax.all_to_all(outgoing, "expert", split_axis=0, concat_axis=0, tiled=True)
    rows = arrived.reshape(-1, width)
    gated = jnp.dot(rows, expert_in[0], preferred_element_type=jnp.float32)
    act = (jax.nn.silu(gated[:, :hidden]) * gated[:, hidden:]).astype(jnp.bfloat16)
    result = jnp.dot(act, expert_out[0], preferred_element_type=jnp.float32).astype(jnp.bfloat16)
    produced = result.reshape(arrived.shape)
    back = lax.all_to_all(produced, "expert", split_axis=0, concat_axis=0, tiled=True)
    own_rows = jnp.dot(
        weighting, back.reshape(-1, width), preferred_element_type=jnp.float32
    ).astype(jnp.bfloat16)
    combined = lax.all_gather(own_rows, "expert", axis=0, tiled=True)
    mixed = jnp.dot(combined, up_proj, preferred_element_type=jnp.float32).astype(jnp.bfloat16)
    partial_grad = jnp.einsum("tl,td->ld", combined, cotangent, preferred_element_type=jnp.float32)
    grad_up = lax.psum(partial_grad, "dp")
    return (mixed, grad_up)


def solution(mesh):
    in_specs = (
        P(("dp", "expert"), None),
        P(None, "expert"),
        P("expert", None, None),
        P("expert", None, None),
        P(("dp", "expert"), None),
        P(("dp", "expert"), None),
        P("dp", "expert"),
    )
    out_specs = (P("dp", "expert"), P(None, "expert"))
    return jax.shard_map(body, mesh=mesh, in_specs=in_specs, out_specs=out_specs, check_vma=False)
```

profile of v0, /device:TPU:1, one launch (start us, length us, event | category | flops | bytes accessed | tf_op | source)
XLA Modules:
  0.0 369.5 jit_solution(11915990606825812268)
XLA Ops:
  7.2 0.0 copy-start
  7.2 0.9 copy.10
  8.1 0.1 eq.62
  8.2 0.1 reshape.94
  8.3 9.0 %reduce-window.6 = s32[32,8,128]{2,1,0:T(8,128)S(1)} reduce-window(s32[32,8,128]{2,1,0:T(8,128)S(1)} %fusion.25, s32[]{:T(128)} %constant.26.clone.1), window={size=1x1x128 pad=0_0x0_0x127_0}, to_apply=%region_0.0 | reduce-window | flops 4161536 | bytes 262148 | tf_op jit(solution)/shard_map/reduce-window
  17.3 0.1 slice.16
  17.4 0.1 copy.12
  17.6 0.1 copy.13
  17.7 0.1 broadcast_add_fusion
  17.8 0.5 fusion.14
  18.4 1.1 convolution_convert_fusion.1
  19.5 0.1 reshape.96
  19.7 53.7 %all_to_all.10 = bf16[32,13,512]{2,1,0:T(8,128)(2,1)S(1)} all-to-all(bf16[32,13,512]{2,1,0:T(8,128)(2,1)S(1)} %reshape.96), channel_id=1, replica_groups=mesh['dp'=32,'expert'=32] {'expert'}, dimensions={0} | all-to-all | bytes 851968 | tf_op jit(solution)/shard_map/all_to_all | solution.py:33
  73.4 0.2 reshape.97
  73.6 4.1 %fusion = f32[416,4096]{1,0:T(8,128)S(1)} fusion(bf16[416,512]{1,0:T(8,128)(2,1)S(1)} %reshape.97, bf16[1,512,4096]{2,1,0:T(8,128)(2,1)} %param.9), kind=kOutput, calls=%fused_computation.1 | convolution fusion | flops 1744830464 | bytes 11436032 | tf_op jit(solution)/shard_map/dot_general | solution.py:35
  77.7 0.0 copy-done
  77.7 0.0 copy-start.2
  77.7 1.1 fusion.8
  78.8 0.9 reshape.98
  79.7 4.0 %all-to-all-start.1 = ((bf16[32,13,512]{2,1,0:T(8,128)(2,1)}), bf16[32,13,512]{2,1,0:T(8,128)(2,1)S(1)}, u32[]{:S(2)}, u32[]{:S(2)}) async-start(bf16[32,13,512]{2,1,0:T(8,128)(2,1)} %reshape.98), calls=%async_computation.1 | async-start | bytes 1048576 | tf_op jit(solution)/shard_map/all_to_all | solution.py:39
  83.8 0.0 all-gather.2.cloned.1.call-start
  83.8 0.0 copy-done.2
  83.8 0.1 copy.9
  84.0 0.1 reshape.100
  84.0 1.4 fusion.13
  85.4 31.9 %all-to-all-done.1 = bf16[32,13,512]{2,1,0:T(8,128)(2,1)S(1)} async-done(((bf16[32,13,512]{2,1,0:T(8,128)(2,1)}), bf16[32,13,512]{2,1,0:T(8,128)(2,1)S(1)}, u32[]{:S(2)}, u32[]{:S(2)}) %all-to-all-start.1) | async-done | bytes 426016 | tf_op jit(solution)/shard_map/all_to_all | solution.py:39
  117.3 0.2 reshape.99
  117.5 0.0 copy-start.1
  117.5 0.9 convolution_convert_fusion.2
  118.4 0.0 all-gather.2.cloned.1.call-update
  118.4 0.0 all-reduce.2.cloned.1.call-start
  118.5 69.4 %all-gather.2.cloned.1.call-done = bf16[4096,512]{1,0:T(8,128)(2,1)} async-done(((bf16[128,512]{1,0:T(8,128)(2,1)}), bf16[4096,512]{1,0:T(8,128)(2,1)}) %all-gather.2.cloned.1.call-update) | async-done | bytes 4194320 | tf_op jit(solution)/shard_map/all_gather | solution.py:43
  187.9 4.5 %fusion.31 = f32[512,128]{1,0:T(8,128)} fusion(bf16[4096,512]{1,0:T(8,128)(2,1)} %all-gather.2.cloned.1.call-done, bf16[4096,128]{1,0:T(8,128)(2,1)} %param.13), kind=kOutput, calls=%fused_computation.41 | convolution fusion | flops 536870912 | bytes 5505024 | tf_op jit(solution)/shard_map/tl,td->ld/dot_general | solution.py:45
  192.4 0.0 all-reduce.2.cloned.1.call-update
  192.4 0.0 copy-done.1
  192.4 4.4 %convolution_convert_fusion = bf16[4096,128]{1,0:T(8,128)(2,1)} fusion(bf16[4096,512]{1,0:T(8,128)(2,1)} %all-gather.2.cloned.1.call-done, bf16[512,128]{1,0:T(8,128)(2,1)S(1)} %copy-done.1), kind=kOutput, calls=%fused_computation | convolution fusion | flops 537395200 | bytes 5373952 | tf_op jit(solution)/shard_map/dot_general | solution.py:44
  196.8 164.1 %all-reduce.2.cloned.1.call-done = f32[512,128]{1,0:T(8,128)} async-done(((f32[512,128]{1,0:T(8,128)}), f32[512,128]{1,0:T(8,128)}) %all-reduce.2.cloned.1.call-update) | async-done | bytes 262160 | tf_op jit(solution)/shard_map/psum | solution.py:46
  360.9 1.7 copy.17
  (5 shorter events, 0.1 us)
Async XLA Ops:
  7.2 70.5 %copy-start = (bf16[1,2048,512]{2,1,0:T(8,128)(2,1)S(1)}, bf16[1,2048,512]{2,1,0:T(8,128)(2,1)}, u32[]{:S(2)}) copy-start(bf16[1,2048,512]{2,1,0:T(8,128)(2,1)} %param.10) | copy-start | bytes 6291460
  77.7 6.1 %copy-start.2 = (bf16[128,8]{0,1:T(8,128)(2,1)S(1)}, bf16[128,8]{0,1:T(8,128)(2,1)}, u32[]{:S(2)}) copy-start(bf16[128,8]{0,1:T(8,128)(2,1)} %param.12) | copy-start | bytes 6148
  79.7 37.6 %all-to-all-start.1 = ((bf16[32,13,512]{2,1,0:T(8,128)(2,1)}), bf16[32,13,512]{2,1,0:T(8,128)(2,1)S(1)}, u32[]{:S(2)}, u32[]{:S(2)}) async-start(bf16[32,13,512]{2,1,0:T(8,128)(2,1)} %reshape.98), calls=%async_computation.1 | async-start | bytes 1048576 | tf_op jit(solution)/shard_map/all_to_all | solution.py:39
  83.8 104.1 %all-gather.2.cloned.1.call-start = ((), (), s32[]{:S(2)}) async-start(), calls=%async_computation.2 | async-start | bytes 4325376 | tf_op jit(solution)/shard_map/all_gather | solution.py:43
  117.5 74.9 %copy-start.1 = (bf16[512,128]{1,0:T(8,128)(2,1)S(1)}, bf16[512,128]{1,0:T(8,128)(2,1)}, u32[]{:S(2)}) copy-start(bf16[512,128]{1,0:T(8,128)(2,1)} %param.8) | copy-start | bytes 393220
  118.4 242.5 %all-reduce.2.cloned.1.call-start = ((), (), s32[]{:S(2)}) async-start(), calls=%async_computation.3 | async-start | bytes 524288 | tf_op jit(solution)/shard_map/psum | solution.py:46
Sparse Core Ops, SparseCore 0:
  118.5 69.3 all-gather.1
  192.5 168.3 all-reduce.1
where the time goes:
time: 373 us; the launch traced here: 369 us
  waiting for transfers between devices  265 us (71%)
  blocking collectives  53.7 us (14%)
  matrix products  18 us (5%)
  between operations  14.2 us (4%)
  other arithmetic  9.21 us (2%)
  local copies, waits for them, and re-layouts  4.7 us (1%)
  starting transfers between devices  4.12 us (1%)
    psum x1, waiting for transfers between devices, body(): grad_up = lax.psum(partial_grad, 'dp')  164 us
    all_gather x1, waiting for transfers between devices, body(): combined = lax.all_gather(own_rows, 'expert', axis=0, tiled=True)  69.4 us
    all_to_all x1, blocking collectives, body(): lax.all_to_all(outgoing, 'expert', split_axis=0, concat_axis=0, tiled=True)  53.7 us
    all_to_all x1, waiting for transfers between devices, body(): lax.all_to_all(produced, 'expert', split_axis=0, concat_axis=0, tiled=True)  31.9 us
    another operation x3, other arithmetic  9.15 us
  transfers between devices with their start and end apart: 3, of which 3 were waited for; matrix products, arithmetic and copies ran while one was open for 2% of the time, Pallas kernels for 0%

commit v1 on v0

v1 whole, which is shorter than its diff:
```python
import jax
import jax.numpy as jnp
from jax import lax
from jax.experimental import pallas as pl
from jax.experimental.pallas import tpu as pltpu
from jax.sharding import PartitionSpec as P

SLOTS = 16
BF16, F32 = jnp.bfloat16, jnp.float32
VMEM = pl.BlockSpec(memory_space=pltpu.VMEM)
LIMIT = pltpu.CompilerParams(vmem_limit_bytes=48 << 20)


def iota(shape, dim):
    return lax.broadcasted_iota(jnp.int32, shape, dim)


def slots_by_row(routes_t, n_expert):
    top, tok = routes_t.shape
    expert = iota((n_expert, tok), 0)
    member = jnp.zeros((n_expert, tok), F32)
    for k in range(top):
        member += jnp.where(routes_t[k : k + 1, :] == expert, 1.0, 0.0)
    earlier = jnp.where(iota((tok, tok), 0) < iota((tok, tok), 1), 1.0, 0.0).astype(BF16)
    slot = jnp.dot(member.astype(BF16), earlier, preferred_element_type=F32)
    slot = jnp.where(member > 0, slot, -1.0).astype(BF16)
    rows = n_expert * SLOTS
    spread = jnp.where(iota((rows, n_expert), 0) // SLOTS == iota((rows, n_expert), 1), 1.0, 0.0).astype(BF16)
    by_row = jnp.dot(spread, slot, preferred_element_type=F32)
    return by_row == (iota((rows, tok), 0) % SLOTS).astype(F32), spread


def dispatch_kernel(routes_ref, latent_ref, out_ref):
    n_expert = out_ref.shape[0] // SLOTS
    takes, _ = slots_by_row(routes_ref[...], n_expert)
    out_ref[...] = jnp.dot(
        jnp.where(takes, 1.0, 0.0).astype(BF16), latent_ref[...], preferred_element_type=F32
    ).astype(BF16)


def weight_kernel(routes_ref, gates_ref, out_ref):
    n_expert = out_ref.shape[1] // SLOTS
    routes_t, gates_t = routes_ref[...], gates_ref[...].astype(F32)
    takes, spread = slots_by_row(routes_t, n_expert)
    top, tok = routes_t.shape
    expert = iota((n_expert, tok), 0)
    gate = jnp.zeros((n_expert, tok), F32)
    for k in range(top):
        gate += jnp.where(routes_t[k : k + 1, :] == expert, gates_t[k : k + 1, :], 0.0)
    by_row = jnp.dot(spread, gate.astype(BF16), preferred_element_type=F32)
    out_ref[...] = jnp.where(takes, by_row, 0.0).T.astype(BF16)


def expert_kernel(x_ref, in_ref, out_w_ref, out_ref):
    hidden = out_w_ref.shape[0]
    step = 512
    x = x_ref[...]
    total = jnp.zeros(out_ref.shape, F32)
    for h in range(0, hidden, step):
        g = jnp.dot(x, in_ref[:, h : h + step], preferred_element_type=F32)
        u = jnp.dot(x, in_ref[:, hidden + h : hidden + h + step], preferred_element_type=F32)
        act = (g / (1.0 + jnp.exp(-g)) * u).astype(BF16)
        total += jnp.dot(act, out_w_ref[h : h + step, :], preferred_element_type=F32)
    out_ref[...] = total.astype(BF16)


def combine_kernel(w_ref, back_ref, out_ref):
    out_ref[...] = jnp.dot(w_ref[...], back_ref[...], preferred_element_type=F32).astype(BF16)


def project_kernel(core_ref, rows_ref, up_ref, cot_ref, *rest):
    before_ref = rest[0] if len(rest) == 5 else None
    mixed_ref, grad_ref, total = rest[-3:]
    i = pl.program_id(0)
    many, tok, width = rows_ref.shape
    rows = rows_ref[...].reshape(many * tok, width)
    cot = cot_ref[...].reshape(many * tok, -1)
    mixed = jnp.dot(rows, up_ref[...], preferred_element_type=F32).astype(BF16)
    mixed_ref[...] = mixed.reshape(mixed_ref.shape)
    part = lax.dot_general(rows, cot, (((0,), (0,)), ((), ())), preferred_element_type=F32)

    @pl.when(i == 0)
    def _():
        total[...] = part if before_ref is None else part + before_ref[...]

    @pl.when(i > 0)
    def _():
        total[...] += part

    @pl.when(i == pl.num_programs(0) - 1)
    def _():
        grad_ref[...] = total[...].astype(grad_ref.dtype)


def project(core, rows, up_proj, cot4, grad=None, mixed=None):
    z, tok, width = rows.shape
    cols = up_proj.shape[1]
    many = z // 4
    first = grad is None
    whole = pl.BlockSpec((width, cols), lambda i, c: (0, 0))
    mine = pl.BlockSpec((many, 1, tok, cols), lambda i, c: (i, c[0], 0, 0))
    in_specs = [pl.BlockSpec((many, tok, width), lambda i, c: (i, 0, 0)), whole, mine]
    args = [core, rows, up_proj, cot4]
    if not first:
        in_specs += [whole, pl.BlockSpec(memory_space=pl.ANY)]
        args += [grad, mixed]
    return pl.pallas_call(
        project_kernel,
        grid_spec=pltpu.PrefetchScalarGridSpec(
            num_scalar_prefetch=1,
            grid=(z // many,),
            in_specs=in_specs,
            out_specs=[mine, whole],
            scratch_shapes=[pltpu.VMEM((width, cols), F32)],
        ),
        out_shape=[
            jax.ShapeDtypeStruct(cot4.shape, BF16),
            jax.ShapeDtypeStruct((width, cols), F32 if first else BF16),
        ],
        input_output_aliases={} if first else {5: 0},
        compiler_params=LIMIT,
        cost_estimate=pl.CostEstimate(flops=4 * z * tok * width * cols, bytes_accessed=4 << 20, transcendentals=0),
        name="project_own" if first else "project_other",
    )(*args)


def body(latent, up_proj, expert_in, expert_out, routes, gates, cotangent):
    n_expert = lax.axis_size("expert")
    n_dp = lax.axis_size("dp")
    tok, width = latent.shape
    cols = up_proj.shape[1]
    nz = n_expert // 2
    slots = n_expert * SLOTS
    same_core = [[z * 2 + c for z in range(nz)] for c in range(2)]
    sds = jax.ShapeDtypeStruct

    routes_t, gates_t = routes.T, gates.T
    outgoing = pl.pallas_call(
        dispatch_kernel, out_shape=sds((slots, width), BF16), in_specs=[VMEM] * 2, out_specs=VMEM, name="dispatch"
    )(routes_t, latent)
    weight = pl.pallas_call(
        weight_kernel, out_shape=sds((tok, slots), BF16), in_specs=[VMEM] * 2, out_specs=VMEM, name="weight"
    )(routes_t, gates_t)
    arrived = lax.all_to_all(
        outgoing.reshape(n_expert, SLOTS, width), "expert", split_axis=0, concat_axis=0, tiled=True
    ).reshape(slots, width)
    produced = pl.pallas_call(
        expert_kernel, out_shape=sds((slots, width), BF16), in_specs=[VMEM] * 3, out_specs=VMEM,
        compiler_params=LIMIT, name="expert",
    )(arrived, expert_in[0], expert_out[0])
    back = lax.all_to_all(
        produced.reshape(n_expert, SLOTS, width), "expert", split_axis=0, concat_axis=0, tiled=True
    ).reshape(slots, width)
    combined = pl.pallas_call(
        combine_kernel, out_shape=sds((tok, width), BF16), in_specs=[VMEM] * 2, out_specs=VMEM, name="combine"
    )(weight, back)

    own = lax.all_gather(combined, "expert", axis=0, tiled=True, axis_index_groups=same_core)
    other = lax.ppermute(own, "expert", [(d, d ^ 1) for d in range(n_expert)])
    core = lax.rem(lax.axis_index("expert"), 2).astype(jnp.int32).reshape(1)
    cot4 = cotangent.reshape(nz, 2, tok, cols)
    mixed, grad = project(core, own.reshape(nz, tok, width), up_proj, cot4)
    mixed, grad = project(1 - core, other.reshape(nz, tok, width), up_proj, cot4, grad, mixed)

    parts = lax.all_to_all(grad.reshape(n_dp, width // n_dp, cols), "dp", split_axis=0, concat_axis=0, tiled=True)
    mine = jnp.sum(parts.astype(F32), axis=0)
    spread = jnp.broadcast_to(mine[None], (n_dp,) + mine.shape)
    grad_up = lax.all_to_all(spread, "dp", split_axis=0, concat_axis=0, tiled=True)
    return mixed.reshape(cotangent.shape), grad_up.reshape(width, cols)


def solution(mesh):
    in_specs = (
        P(("dp", "expert"), None),
        P(None, "expert"),
        P("expert", None, None),
        P("expert", None, None),
        P(("dp", "expert"), None),
        P(("dp", "expert"), None),
        P("dp", "expert"),
    )
    out_specs = (P("dp", "expert"), P(None, "expert"))
    return jax.shard_map(body, mesh=mesh, in_specs=in_specs, out_specs=out_specs, check_vma=False)
```

time: 373 us -> 233 us (0.62)
  waiting for transfers between devices: 265 us -> 90.8 us
  blocking collectives: 53.7 us -> 86.7 us
  Pallas kernels: 0 us -> 18.4 us
  matrix products: 18 us -> 0 us
  starting transfers between devices: 4.12 us -> 16.1 us
  other arithmetic: 9.21 us -> 0.04 us
    psum x1 -> x0, waiting for transfers between devices: 164 us -> none  [body(): grad_up = lax.psum(partial_grad, 'dp')]
    all_to_all x1 -> x3, blocking collectives: 53.7 us -> 86.7 us  [the longest x1 53.9 us: body(): lax.all_to_all(outgoing.reshape(n_expert, SLOTS, width), 'expert', split_...]
    pallas_call x0 -> x6, Pallas kernels: none -> 18.4 us  [the longest x1 6.74 us: body(): pl.pallas_call(expert_kernel, out_shape=sds((slots, width), BF16), in_spe...]
    dot_general x8 -> x0, matrix products: 18 us -> none  [the longest x1 4.47 us: body(): jnp.einsum('tl,td->ld', combined, cotangent, preferred_element_type=jnp.f...]
    ppermute x0 -> x1, starting transfers between devices: none -> 11.9 us  [body(): other = lax.ppermute(own, 'expert', [(d, d ^ 1) for d in range(n_expert)])]
    all_gather x1, waiting for transfers between devices: 69.4 us -> 59.1 us  [body(): lax.all_gather(combined, 'expert', axis=0, tiled=True, axis_index_groups=...]
    another operation x3 -> x0, other arithmetic: 9.15 us -> none
  transfers between devices with their start and end apart: 3 -> 3, of which waited for: 3 -> 2; matrix products, arithmetic and copies ran while one was open for 2% -> 0% of each run, Pallas kernels for 0% -> 2%
where the time goes in v1:
time: 233 us; the launch traced here: 231 us
  waiting for transfers between devices  90.8 us (39%)
  blocking collectives  86.7 us (37%)
  Pallas kernels  18.4 us (8%)
  starting transfers between devices  16.1 us (7%)
  between operations  14.1 us (6%)
  local copies, waits for them, and re-layouts  4.7 us (2%)
    all_gather x1, waiting for transfers between devices, body(): lax.all_gather(combined, 'expert', axis=0, tiled=True, axis_index_groups=...  59.1 us
    all_to_all x1, blocking collectives, body(): lax.all_to_all(outgoing.reshape(n_expert, SLOTS, width), 'expert', split_...  53.9 us
    all_to_all x1, waiting for transfers between devices, body(): lax.all_to_all(produced.reshape(n_expert, SLOTS, width), 'expert', split_...  31.7 us
    all_to_all x1, blocking collectives, body(): lax.all_to_all(grad.reshape(n_dp, width // n_dp, cols), 'dp', split_axis=...  19 us
    all_to_all x1, blocking collectives, body(): lax.all_to_all(spread, 'dp', split_axis=0, concat_axis=0, tiled=True)  13.8 us
    ppermute x1, starting transfers between devices, body(): other = lax.ppermute(own, 'expert', [(d, d ^ 1) for d in range(n_expert)])  11.9 us
    pallas_call x1, Pallas kernels, body(): pl.pallas_call(expert_kernel, out_shape=sds((slots, width), BF16), in_spe...  6.74 us
    pallas_call x2, Pallas kernels, project(): pl.pallas_call(project_kernel, grid_spec=pltpu.PrefetchScalarGridSpec(num...  5.67 us
  transfers between devices with their start and end apart: 3, of which 2 were waited for; matrix products, arithmetic and copies ran while one was open for 0% of the time, Pallas kernels for 2%

profile of v1, /device:TPU:1, one launch (start us, length us, event | category | flops | bytes accessed | tf_op | source)
XLA Modules:
  0.0 230.9 jit_solution(885210005864781174)
XLA Ops:
  7.2 2.2 dispatch.1
  9.4 53.9 %all_to_all.20 = bf16[32,16,512]{2,1,0:T(8,128)(2,1)S(1)} all-to-all(bf16[32,16,512]{2,1,0:T(8,128)(2,1)} %bitcast.23), channel_id=1, replica_groups=mesh['dp'=32,'expert'=32] {'expert'}, dimensions={0} | all-to-all | bytes 1048576 | tf_op jit(solution)/shard_map/all_to_all | solution.py:144
  63.3 0.0 copy-start.1
  63.3 1.6 copy-done.1
  64.9 6.7 %expert.1 = bf16[512,512]{1,0:T(8,128)(2,1)} custom-call(bf16[512,512]{1,0:T(8,128)(2,1)S(1)} %bitcast.17, bf16[512,4096]{1,0:T(8,128)(2,1)} %bitcast.22, bf16[2048,512]{1,0:T(8,128)(2,1)S(1)} %bitcast.18), custom_call_target="tpu_custom_call" | custom-call | tf_op jit(solution)/shard_map/expert/pallas_call | solution.py:147
  71.7 0.0 copy-start
  71.7 0.0 copy-start.3
  71.7 4.2 %all-to-all-start.1 = ((bf16[32,16,512]{2,1,0:T(8,128)(2,1)}), bf16[32,16,512]{2,1,0:T(8,128)(2,1)S(1)}, u32[]{:S(2)}, u32[]{:S(2)}) async-start(bf16[32,16,512]{2,1,0:T(8,128)(2,1)} %bitcast.7), calls=%async_computation.1 | async-start | bytes 1048576 | tf_op jit(solution)/shard_map/all_to_all | solution.py:151
  75.8 0.0 all-gather.2.cloned.1.call-start
  75.9 1.8 weight.1.w_ref
  77.7 31.7 %all-to-all-done.1 = bf16[32,16,512]{2,1,0:T(8,128)(2,1)S(1)} async-done(((bf16[32,16,512]{2,1,0:T(8,128)(2,1)}), bf16[32,16,512]{2,1,0:T(8,128)(2,1)S(1)}, u32[]{:S(2)}, u32[]{:S(2)}) %all-to-all-start.1) | async-done | bytes 524320 | tf_op jit(solution)/shard_map/all_to_all | solution.py:151
  109.4 0.0 copy-start.4
  109.4 0.8 copy-done.4
  110.2 2.0 combine.1
  112.2 0.0 all-gather.2.cloned.1.call-update
  112.2 59.1 %all-gather.2.cloned.1.call-done = bf16[2048,512]{1,0:T(8,128)(2,1)} async-done(((bf16[128,512]{1,0:T(8,128)(2,1)}), bf16[2048,512]{1,0:T(8,128)(2,1)}) %all-gather.2.cloned.1.call-update) | async-done | bytes 2097168 | tf_op jit(solution)/shard_map/all_gather | solution.py:158
  171.3 11.9 %collective-permute-start = (bf16[2048,512]{1,0:T(8,128)(2,1)}, bf16[2048,512]{1,0:T(8,128)(2,1)S(1)}, u32[]{:S(2)}, u32[]{:S(2)}) collective-permute-start(bf16[2048,512]{1,0:T(8,128)(2,1)} %all-gather.2.cloned.1.call-done), channel_id=1, source_target_pairs={{0,1},{1,0},{2,3},{3,2},{4,5},{5,4},{6,7},{7,6},{8,9},{9,8},{10,11... | collective-permute-start | bytes 6291464 | tf_op jit(solution)/shard_map/ppermute | solution.py:159
  183.2 0.0 copy-done
  183.2 0.0 copy-done.3
  183.2 0.0 copy-start.2
  183.2 1.6 copy-done.2
  184.8 2.8 %project_own.1 = (bf16[16,2,128,128]{3,2,1,0:T(8,128)(2,1)}, f32[512,128]{1,0:T(8,128)S(1)}) custom-call(s32[1]{0:T(128)} %bitcast.core_ref, bf16[16,128,512]{2,1,0:T(8,128)(2,1)S(1)} %bitcast.20, bf16[512,128]{1,0:T(8,128)(2,1)S(1)} %copy-done.3, bf16[16,2,128,128]{3,2,1,0:T(8,128)(2,1)S(1)} %bitcast.15), custom_call_target="tpu_custom_call" | custom-call | flops 536870912 | bytes 4194304 | tf_op jit(solution)/shard_map/project_own/pallas_call | solution.py:107
  187.6 0.0 collective-permute-done
  187.6 2.8 %project_other.1 = (bf16[16,2,128,128]{3,2,1,0:T(8,128)(2,1)}, bf16[512,128]{1,0:T(8,128)(2,1)S(1)}) custom-call(s32[1]{0:T(128)S(6)} %sub.3.core_ref, bf16[16,128,512]{2,1,0:T(8,128)(2,1)S(1)} %bitcast.19, bf16[512,128]{1,0:T(8,128)(2,1)S(1)} %copy-done.3, bf16[16,2,128,128]{3,2,1,0:T(8,128)(2,1)S(1)} %bitcast.16, ...), custom_call_target="tpu_custom_call", output_to_operand_aliasing={{0}: (5, {})} | custom-call | flops 536870912 | bytes 4194304 | tf_op jit(solution)/shard_map/project_other/pallas_call | solution.py:107
  190.5 19.0 %all_to_all.21 = bf16[32,16,128]{2,1,0:T(8,128)(2,1)S(1)} all-to-all(bf16[32,16,128]{2,1,0:T(8,128)(2,1)S(1)} %bitcast.21), channel_id=1, replica_groups=mesh['dp'=32,'expert'=32] {'dp'}, dimensions={0} | all-to-all | bytes 262144 | tf_op jit(solution)/shard_map/all_to_all | solution.py:165
  209.6 13.8 %all_to_all.22 = f32[32,16,128]{2,1,0:T(8,128)S(1)} all-to-all(f32[32,16,128]{2,1,0:T(8,128)S(1)} %broadcast_in_dim.2), channel_id=1, replica_groups=mesh['dp'=32,'expert'=32] {'dp'}, dimensions={0} | all-to-all | bytes 524288 | tf_op jit(solution)/shard_map/all_to_all | solution.py:168
  223.4 0.7 copy.12
  (2 shorter events, 0.1 us)
Async XLA Ops:
  63.3 1.6 copy-start.1
  71.7 111.5 %copy-start = (bf16[4096,128]{1,0:T(8,128)(2,1)S(1)}, bf16[4096,128]{1,0:T(8,128)(2,1)}, u32[]{:S(2)}) copy-start(bf16[4096,128]{1,0:T(8,128)(2,1)} %param.13) | copy-start | bytes 3145732
  71.7 111.5 %copy-start.3 = (bf16[512,128]{1,0:T(8,128)(2,1)S(1)}, bf16[512,128]{1,0:T(8,128)(2,1)}, u32[]{:S(2)}) copy-start(bf16[512,128]{1,0:T(8,128)(2,1)} %up_ref.3) | copy-start | bytes 393220
  71.7 37.7 %all-to-all-start.1 = ((bf16[32,16,512]{2,1,0:T(8,128)(2,1)}), bf16[32,16,512]{2,1,0:T(8,128)(2,1)S(1)}, u32[]{:S(2)}, u32[]{:S(2)}) async-start(bf16[32,16,512]{2,1,0:T(8,128)(2,1)} %bitcast.7), calls=%async_computation.1 | async-start | bytes 1048576 | tf_op jit(solution)/shard_map/all_to_all | solution.py:151
  75.8 95.4 %all-gather.2.cloned.1.call-start = ((), (), s32[]{:S(2)}) async-start(), calls=%async_computation.4 | async-start | bytes 2228224 | tf_op jit(solution)/shard_map/all_gather | solution.py:158
  109.4 0.8 copy-start.4
  171.3 16.4 %collective-permute-start = (bf16[2048,512]{1,0:T(8,128)(2,1)}, bf16[2048,512]{1,0:T(8,128)(2,1)S(1)}, u32[]{:S(2)}, u32[]{:S(2)}) collective-permute-start(bf16[2048,512]{1,0:T(8,128)(2,1)} %all-gather.2.cloned.1.call-done), channel_id=1, source_target_pairs={{0,1},{1,0},{2,3},{3,2},{4,5},{5,4},{6,7},{7,6},{8,9},{9,8},{10,11... | collective-permute-start | bytes 6291464 | tf_op jit(solution)/shard_map/ppermute | solution.py:159
  183.2 1.6 copy-start.2
Sparse Core Ops, SparseCore 0:
  112.3 58.8 all-gather.1

commit v2 on v1

v2 whole, which is shorter than its diff:
```python
import jax
import jax.numpy as jnp
from jax import lax
from jax.experimental import pallas as pl
from jax.experimental.pallas import tpu as pltpu
from jax.sharding import PartitionSpec as P

SLOTS = 16
EXTRA = 8
BF16, F32 = jnp.bfloat16, jnp.float32
VMEM = pl.BlockSpec(memory_space=pltpu.VMEM)
LIMIT = pltpu.CompilerParams(vmem_limit_bytes=48 << 20)


def iota(shape, dim):
    return lax.broadcasted_iota(jnp.int32, shape, dim)


def slots_by_row(routes_t, n_expert):
    top, tok = routes_t.shape
    expert = iota((n_expert, tok), 0)
    member = jnp.zeros((n_expert, tok), F32)
    for k in range(top):
        member += jnp.where(routes_t[k : k + 1, :] == expert, 1.0, 0.0)
    earlier = jnp.where(iota((tok, tok), 0) < iota((tok, tok), 1), 1.0, 0.0).astype(BF16)
    slot = jnp.dot(member.astype(BF16), earlier, preferred_element_type=F32)
    slot = jnp.where(member > 0, slot, -1.0).astype(BF16)
    rows = n_expert * SLOTS
    spread = jnp.where(iota((rows, n_expert), 0) // SLOTS == iota((rows, n_expert), 1), 1.0, 0.0).astype(BF16)
    by_row = jnp.dot(spread, slot, preferred_element_type=F32)
    return by_row == (iota((rows, tok), 0) % SLOTS).astype(F32), spread


def dispatch_kernel(routes_ref, latent_ref, out_ref):
    n_expert = out_ref.shape[0] // SLOTS
    takes, _ = slots_by_row(routes_ref[...], n_expert)
    out_ref[...] = jnp.dot(
        jnp.where(takes, 1.0, 0.0).astype(BF16), latent_ref[...], preferred_element_type=F32
    ).astype(BF16)


def weight_kernel(routes_ref, gates_ref, out_ref):
    n_expert = out_ref.shape[1] // SLOTS
    routes_t, gates_t = routes_ref[...], gates_ref[...].astype(F32)
    takes, spread = slots_by_row(routes_t, n_expert)
    top, tok = routes_t.shape
    expert = iota((n_expert, tok), 0)
    gate = jnp.zeros((n_expert, tok), F32)
    for k in range(top):
        gate += jnp.where(routes_t[k : k + 1, :] == expert, gates_t[k : k + 1, :], 0.0)
    by_row = jnp.dot(spread, gate.astype(BF16), preferred_element_type=F32)
    out_ref[...] = jnp.where(takes, by_row, 0.0).T.astype(BF16)


def expert_kernel(x_ref, in_hbm, out_hbm, out_ref, in_ref, out_w_ref, sems):
    hidden = out_w_ref.shape[0]
    step = hidden // sems.shape[0]
    copies = []
    for n in range(sems.shape[0]):
        gate, up = pl.ds(n * step, step), pl.ds(hidden + n * step, step)
        group = [
            pltpu.make_async_copy(in_hbm.at[:, gate], in_ref.at[:, gate], sems.at[n, 0]),
            pltpu.make_async_copy(in_hbm.at[:, up], in_ref.at[:, up], sems.at[n, 1]),
            pltpu.make_async_copy(out_hbm.at[gate, :], out_w_ref.at[gate, :], sems.at[n, 2]),
        ]
        for copy in group:
            copy.start()
        copies.append(group)
    x = x_ref[...]
    total = jnp.zeros(out_ref.shape, F32)
    for n, group in enumerate(copies):
        h = n * step
        group[0].wait()
        g = jnp.dot(x, in_ref[:, h : h + step], preferred_element_type=F32)
        group[1].wait()
        u = jnp.dot(x, in_ref[:, hidden + h : hidden + h + step], preferred_element_type=F32)
        act = (g / (1.0 + jnp.exp(-g)) * u).astype(BF16)
        group[2].wait()
        total += jnp.dot(act, out_w_ref[h : h + step, :], preferred_element_type=F32)
    out_ref[...] = total.astype(BF16)


def power(e):
    return jnp.exp2(e).astype(BF16)


def combine_kernel(w_ref, back_ref, out_ref):
    tok = w_ref.shape[0]
    combined = jnp.dot(w_ref[...], back_ref[...], preferred_element_type=F32).astype(BF16).astype(F32)
    largest = jnp.maximum(jnp.max(jnp.abs(combined), axis=1, keepdims=True), 2.0**-100)
    e = jnp.floor(jnp.log2(largest) + 1e-4) - 14.0
    whole = jnp.round(combined * power(-e).astype(F32))
    out_ref[0, :tok, :] = whole.astype(jnp.int32).astype(jnp.int16)
    across = jnp.broadcast_to(e, (tok, tok)).T[:EXTRA]
    out_ref[0, tok:, :] = jnp.concatenate([across] * (combined.shape[1] // tok), axis=1).astype(jnp.int32).astype(jnp.int16)


def chunk_copy(coded_hbm, coded_ref, sems, i):
    many = coded_ref.shape[0] // sems.shape[0]
    part = pl.ds(i * many, many)
    return pltpu.make_async_copy(coded_hbm.at[part], coded_ref.at[part], sems.at[i])


def rows_and_scales(coded_ref, n, tok):
    coded = coded_ref[n].astype(jnp.int32).astype(F32)
    scale = power(coded[tok : tok + 1, :tok]).astype(F32)
    diagonal = jnp.where(iota((tok, tok), 0) == iota((tok, tok), 1), jnp.broadcast_to(scale, (tok, tok)), 0.0)
    return coded[:tok].astype(BF16), diagonal.astype(BF16)


def grad_kernel(coded_hbm, cot_ref, out_ref, total, coded_ref, sems):
    sources, chunks = coded_ref.shape[0], sems.shape[0]
    tok = cot_ref.shape[0] // sources
    many = sources // chunks
    for i in range(chunks):
        chunk_copy(coded_hbm, coded_ref, sems, i).start()
    total[...] = jnp.zeros_like(total)

    def step(i, carry):
        chunk_copy(coded_hbm, coded_ref, sems, i).wait()
        rows, cots = [], []
        for j in range(many):
            n = i * many + j
            coded, diagonal = rows_and_scales(coded_ref, n, tok)
            cot = cot_ref[pl.ds(pl.multiple_of(n * tok, tok), tok), :]
            rows.append(coded)
            cots.append(jnp.dot(diagonal, cot, preferred_element_type=F32).astype(BF16))
        total[...] += lax.dot_general(
            jnp.concatenate(cots), jnp.concatenate(rows), (((0,), (0,)), ((), ())), preferred_element_type=F32
        )
        return carry

    lax.fori_loop(0, chunks, step, 0)
    out_ref[...] = total[...].T.astype(BF16)


def mixed_kernel(coded_hbm, up_ref, out_ref, coded_ref, sems):
    sources, chunks = coded_ref.shape[0], sems.shape[0]
    tok = out_ref.shape[0] // sources
    many = sources // chunks
    for i in range(chunks):
        chunk_copy(coded_hbm, coded_ref, sems, i).start()
    ones = jnp.ones((tok, out_ref.shape[1]), BF16)

    def step(i, carry):
        chunk_copy(coded_hbm, coded_ref, sems, i).wait()
        for j in range(many):
            n = i * many + j
            coded, diagonal = rows_and_scales(coded_ref, n, tok)
            scale = jnp.dot(diagonal, ones, preferred_element_type=F32)
            mixed = jnp.dot(coded, up_ref[...], preferred_element_type=F32) * scale
            out_ref[pl.ds(pl.multiple_of(n * tok, tok), tok), :] = mixed.astype(BF16)
        return carry

    lax.fori_loop(0, chunks, step, 0)


def body(latent, up_proj, expert_in, expert_out, routes, gates, cotangent):
    n_expert = lax.axis_size("expert")
    n_dp = lax.axis_size("dp")
    tok, width = latent.shape
    cols = up_proj.shape[1]
    slots = n_expert * SLOTS
    sds = jax.ShapeDtypeStruct

    routes_t, gates_t = routes.T, gates.T
    outgoing = pl.pallas_call(
        dispatch_kernel, out_shape=sds((slots, width), BF16), in_specs=[VMEM] * 2, out_specs=VMEM, name="dispatch"
    )(routes_t, latent)
    weight = pl.pallas_call(
        weight_kernel, out_shape=sds((tok, slots), BF16), in_specs=[VMEM] * 2, out_specs=VMEM, name="weight"
    )(routes_t, gates_t)
    arrived = lax.all_to_all(
        outgoing.reshape(n_expert, SLOTS, width), "expert", split_axis=0, concat_axis=0, tiled=True
    ).reshape(slots, width)
    hidden = expert_out.shape[1]
    hbm = pl.BlockSpec(memory_space=pltpu.HBM)
    produced = pl.pallas_call(
        expert_kernel, out_shape=sds((slots, width), BF16), in_specs=[VMEM, hbm, hbm], out_specs=VMEM,
        scratch_shapes=[
            pltpu.VMEM((width, 2 * hidden), BF16),
            pltpu.VMEM((hidden, width), BF16),
            pltpu.SemaphoreType.DMA((4, 3)),
        ],
        compiler_params=LIMIT, name="expert",
    )(arrived, expert_in[0], expert_out[0])
    back = lax.all_to_all(
        produced.reshape(n_expert, SLOTS, width), "expert", split_axis=0, concat_axis=0, tiled=True
    ).reshape(slots, width)
    coded = pl.pallas_call(
        combine_kernel, out_shape=sds((1, tok + EXTRA, width), jnp.int16), in_specs=[VMEM] * 2, out_specs=VMEM,
        compiler_params=LIMIT, name="combine",
    )(weight, back)
    gathered = lax.all_gather(coded, "expert", axis=0, tiled=True)
    chunks = [pltpu.VMEM(gathered.shape, gathered.dtype), pltpu.SemaphoreType.DMA((n_expert // 4,))]
    grad = pl.pallas_call(
        grad_kernel, out_shape=sds((width, cols), BF16), in_specs=[hbm, VMEM], out_specs=VMEM,
        scratch_shapes=[pltpu.VMEM((cols, width), F32)] + chunks, compiler_params=LIMIT, name="grad",
    )(gathered, cotangent)
    mixed = pl.pallas_call(
        mixed_kernel, out_shape=sds(cotangent.shape, BF16), in_specs=[hbm, VMEM], out_specs=VMEM,
        scratch_shapes=chunks,
        compiler_params=LIMIT, name="mixed",
        cost_estimate=pl.CostEstimate(flops=2 * cotangent.shape[0] * width * cols, bytes_accessed=6 << 20, transcendentals=0),
    )(gathered, up_proj)

    parts = lax.all_to_all(grad.reshape(n_dp, width // n_dp, cols), "dp", split_axis=0, concat_axis=0, tiled=True)
    mine = jnp.sum(parts.astype(F32), axis=0)
    spread = jnp.broadcast_to(mine[None], (n_dp,) + mine.shape)
    grad_up = lax.all_to_all(spread, "dp", split_axis=0, concat_axis=0, tiled=True)
    return mixed, grad_up.reshape(width, cols)


def solution(mesh):
    in_specs = (
        P(("dp", "expert"), None),
        P(None, "expert"),
        P("expert", None, None),
        P("expert", None, None),
        P(("dp", "expert"), None),
        P(("dp", "expert"), None),
        P("dp", "expert"),
    )
    out_specs = (P("dp", "expert"), P(None, "expert"))
    return jax.shard_map(body, mesh=mesh, in_specs=in_specs, out_specs=out_specs, check_vma=False)
```

time: 233 us -> 192 us (0.82)
  waiting for transfers between devices: 90.8 us -> 35.6 us
  blocking collectives: 86.7 us -> 118 us
  between operations: 14.1 us -> 0.71 us
  starting transfers between devices: 16.1 us -> 8.04 us
  local copies, waits for them, and re-layouts: 4.7 us -> 8.19 us
    all_gather x1 -> x0, waiting for transfers between devices: 59.1 us -> none  [body(): lax.all_gather(combined, 'expert', axis=0, tiled=True, axis_index_groups=...]
    all_gather x0 -> x1, blocking collectives: none -> 44.3 us  [body(): gathered = lax.all_gather(coded, 'expert', axis=0, tiled=True)]
    all_to_all x1 -> x0, blocking collectives: 13.8 us -> none  [body(): lax.all_to_all(spread, 'dp', split_axis=0, concat_axis=0, tiled=True)]
    ppermute x1 -> x0, starting transfers between devices: 11.9 us -> none  [body(): other = lax.ppermute(own, 'expert', [(d, d ^ 1) for d in range(n_expert)])]
    all_to_all x0 -> x1, starting transfers between devices: none -> 3.87 us  [body(): lax.all_to_all(spread, 'dp', split_axis=0, concat_axis=0, tiled=True)]
    all_to_all x0 -> x1, waiting for transfers between devices: none -> 3.79 us  [body(): lax.all_to_all(spread, 'dp', split_axis=0, concat_axis=0, tiled=True)]
    unnamed x11 -> x13, local copies, waits for them, and re-layouts: 4.68 us -> 7.47 us
  transfers between devices with their start and end apart: 3 -> 2, of which waited for: 2 -> 2; matrix products, arithmetic and copies ran while one was open for 0% -> 0% of each run, Pallas kernels for 2% -> 3%
where the time goes in v2:
time: 192 us; the launch traced here: 190 us
  blocking collectives  118 us (61%)
  waiting for transfers between devices  35.6 us (19%)
  Pallas kernels  19.9 us (10%)
  local copies, waits for them, and re-layouts  8.19 us (4%)
  starting transfers between devices  8.04 us (4%)
    all_to_all x1, blocking collectives, body(): lax.all_to_all(outgoing.reshape(n_expert, SLOTS, width), 'expert', split_...  53.9 us
    all_gather x1, blocking collectives, body(): gathered = lax.all_gather(coded, 'expert', axis=0, tiled=True)  44.3 us
    all_to_all x1, waiting for transfers between devices, body(): lax.all_to_all(produced.reshape(n_expert, SLOTS, width), 'expert', split_...  31.8 us
    all_to_all x1, blocking collectives, body(): lax.all_to_all(grad.reshape(n_dp, width // n_dp, cols), 'dp', split_axis=...  19.3 us
    unnamed x13, local copies, waits for them, and re-layouts  7.47 us
    pallas_call x1, Pallas kernels, body(): pl.pallas_call(expert_kernel, out_shape=sds((slots, width), BF16), in_spe...  7.14 us
    pallas_call x1, Pallas kernels, body(): pl.pallas_call(mixed_kernel, out_shape=sds(cotangent.shape, BF16), in_spe...  4.29 us
    all_to_all x1, starting transfers between devices, body(): lax.all_to_all(produced.reshape(n_expert, SLOTS, width), 'expert', split_...  4.17 us
  transfers between devices with their start and end apart: 2, of which 2 were waited for; matrix products, arithmetic and copies ran while one was open for 0% of the time, Pallas kernels for 3%

profile of v2, /device:TPU:1, one launch (start us, length us, event | category | flops | bytes accessed | tf_op | source)
XLA Modules:
  0.0 189.9 jit_solution(7756351855154592635)
XLA Ops:
  0.6 2.2 %dispatch.1 = bf16[512,512]{1,0:T(8,128)(2,1)} custom-call(s32[8,128]{1,0:T(8,128)} %bitcast.17, bf16[128,512]{1,0:T(8,128)(2,1)} %latent_ref.1), custom_call_target="tpu_custom_call" | custom-call | tf_op jit(solution)/shard_map/dispatch/pallas_call | solution.py:167
  2.9 53.9 %all_to_all.20 = bf16[32,16,512]{2,1,0:T(8,128)(2,1)S(1)} all-to-all(bf16[32,16,512]{2,1,0:T(8,128)(2,1)} %bitcast.15), channel_id=1, replica_groups=mesh['dp'=32,'expert'=32] {'expert'}, dimensions={0} | all-to-all | bytes 1048576 | tf_op jit(solution)/shard_map/all_to_all | solution.py:173
  56.8 0.0 copy-start.2
  56.8 1.6 copy-done.2
  58.4 7.1 %expert.1 = bf16[512,512]{1,0:T(8,128)(2,1)} custom-call(bf16[512,512]{1,0:T(8,128)(2,1)S(1)} %bitcast.10, bf16[512,4096]{1,0:T(8,128)(2,1)} %bitcast.14, bf16[2048,512]{1,0:T(8,128)(2,1)S(1)} %bitcast.11), custom_call_target="tpu_custom_call" | custom-call | tf_op jit(solution)/shard_map/expert/pallas_call | solution.py:178
  65.5 0.0 copy-start.3
  65.5 4.2 %all-to-all-start.1 = ((bf16[32,16,512]{2,1,0:T(8,128)(2,1)}), bf16[32,16,512]{2,1,0:T(8,128)(2,1)S(1)}, u32[]{:S(2)}, u32[]{:S(2)}) async-start(bf16[32,16,512]{2,1,0:T(8,128)(2,1)} %bitcast.6), calls=%async_computation.1 | async-start | bytes 1048576 | tf_op jit(solution)/shard_map/all_to_all | solution.py:187
  69.7 1.8 weight.1.w_ref
  71.5 31.8 %all-to-all-done.1 = bf16[32,16,512]{2,1,0:T(8,128)(2,1)S(1)} async-done(((bf16[32,16,512]{2,1,0:T(8,128)(2,1)}), bf16[32,16,512]{2,1,0:T(8,128)(2,1)S(1)}, u32[]{:S(2)}, u32[]{:S(2)}) %all-to-all-start.1) | async-done | bytes 524320 | tf_op jit(solution)/shard_map/all_to_all | solution.py:187
  103.3 0.0 copy-start.4
  103.3 0.9 copy-done.4
  104.2 0.4 combine.1
  104.6 44.3 %all-gather.1.coded_hbm = s16[32,136,512]{2,1,0:T(8,128)(2,1)S(1)} all-gather(s16[1,136,512]{2,1,0:T(8,128)(2,1)S(1)} %combine.1), channel_id=1, replica_groups=mesh['dp'=32,'expert'=32] {'expert'}, dimensions={0}, use_global_device_ids=true | all-gather | bytes 4595712 | tf_op jit(solution)/shard_map/all_gather | solution.py:194
  148.9 0.0 copy-done.3
  148.9 0.0 copy-start.5
  148.9 4.0 %grad.1 = bf16[512,128]{1,0:T(8,128)(2,1)S(1)} custom-call(s16[32,136,512]{2,1,0:T(8,128)(2,1)S(1)} %all-gather.1.coded_hbm, bf16[4096,128]{1,0:T(8,128)(2,1)S(1)} %copy-done.3), custom_call_target="tpu_custom_call" | custom-call | tf_op jit(solution)/shard_map/grad/pallas_call | solution.py:196
  152.9 0.0 copy-start
  152.9 2.0 %copy-done = s16[32,136,512]{2,1,0:T(8,128)(2,1)} copy-done((s16[32,136,512]{2,1,0:T(8,128)(2,1)}, s16[32,136,512]{2,1,0:T(8,128)(2,1)S(1)}, u32[]{:S(2)}) %copy-start) | copy-done | bytes 4456472
  154.9 19.3 %all_to_all.21 = bf16[32,16,128]{2,1,0:T(8,128)(2,1)S(1)} all-to-all(bf16[32,16,128]{2,1,0:T(8,128)(2,1)S(1)} %bitcast.13), channel_id=1, replica_groups=mesh['dp'=32,'expert'=32] {'dp'}, dimensions={0} | all-to-all | bytes 262144 | tf_op jit(solution)/shard_map/all_to_all | solution.py:207
  174.3 0.7 broadcast_in_dim.2
  175.0 3.9 %all-to-all-start.3 = ((f32[32,16,128]{2,1,0:T(8,128)}), f32[32,16,128]{2,1,0:T(8,128)S(1)}, u32[]{:S(2)}, u32[]{:S(2)}) async-start(f32[32,16,128]{2,1,0:T(8,128)} %broadcast_in_dim.2), calls=%async_computation.3 | async-start | bytes 524288 | tf_op jit(solution)/shard_map/all_to_all | solution.py:210
  178.9 0.0 copy-done.5
  178.9 0.0 copy-start.1
  178.9 2.3 %copy-done.1 = s16[32,136,512]{2,1,0:T(8,128)(2,1)S(1)} copy-done((s16[32,136,512]{2,1,0:T(8,128)(2,1)S(1)}, s16[32,136,512]{2,1,0:T(8,128)(2,1)}, u32[]{:S(2)}) %copy-start.1) | copy-done | bytes 4456472
  181.1 4.3 %mixed.1 = bf16[4096,128]{1,0:T(8,128)(2,1)} custom-call(s16[32,136,512]{2,1,0:T(8,128)(2,1)S(1)} %copy-done.1, bf16[512,128]{1,0:T(8,128)(2,1)S(1)} %copy-done.5), custom_call_target="tpu_custom_call" | custom-call | flops 536870912 | bytes 6291456 | tf_op jit(solution)/shard_map/mixed/pallas_call | solution.py:200
  185.4 3.8 %all-to-all-done.3 = f32[32,16,128]{2,1,0:T(8,128)S(1)} async-done(((f32[32,16,128]{2,1,0:T(8,128)}), f32[32,16,128]{2,1,0:T(8,128)S(1)}, u32[]{:S(2)}, u32[]{:S(2)}) %all-to-all-start.3) | async-done | bytes 262176 | tf_op jit(solution)/shard_map/all_to_all | solution.py:210
  189.2 0.7 copy.10
  (1 shorter events, 0.0 us)
Async XLA Ops:
  56.8 1.6 copy-start.2
  65.5 83.3 %copy-start.3 = (bf16[4096,128]{1,0:T(8,128)(2,1)S(1)}, bf16[4096,128]{1,0:T(8,128)(2,1)}, u32[]{:S(2)}) copy-start(bf16[4096,128]{1,0:T(8,128)(2,1)} %cot_ref.1) | copy-start | bytes 3145732
  65.5 37.7 %all-to-all-start.1 = ((bf16[32,16,512]{2,1,0:T(8,128)(2,1)}), bf16[32,16,512]{2,1,0:T(8,128)(2,1)S(1)}, u32[]{:S(2)}, u32[]{:S(2)}) async-start(bf16[32,16,512]{2,1,0:T(8,128)(2,1)} %bitcast.6), calls=%async_computation.1 | async-start | bytes 1048576 | tf_op jit(solution)/shard_map/all_to_all | solution.py:187
  103.3 0.9 copy-start.4
  148.9 30.0 %copy-start.5 = (bf16[512,128]{1,0:T(8,128)(2,1)S(1)}, bf16[512,128]{1,0:T(8,128)(2,1)}, u32[]{:S(2)}) copy-start(bf16[512,128]{1,0:T(8,128)(2,1)} %up_ref.1) | copy-start | bytes 393220
  152.9 2.0 %copy-start = (s16[32,136,512]{2,1,0:T(8,128)(2,1)}, s16[32,136,512]{2,1,0:T(8,128)(2,1)S(1)}, u32[]{:S(2)}) copy-start(s16[32,136,512]{2,1,0:T(8,128)(2,1)S(1)} %all-gather.1.coded_hbm) | copy-start | bytes 13369348
  175.0 14.2 %all-to-all-start.3 = ((f32[32,16,128]{2,1,0:T(8,128)}), f32[32,16,128]{2,1,0:T(8,128)S(1)}, u32[]{:S(2)}, u32[]{:S(2)}) async-start(f32[32,16,128]{2,1,0:T(8,128)} %broadcast_in_dim.2), calls=%async_computation.3 | async-start | bytes 524288 | tf_op jit(solution)/shard_map/all_to_all | solution.py:210
  178.9 2.3 %copy-start.1 = (s16[32,136,512]{2,1,0:T(8,128)(2,1)S(1)}, s16[32,136,512]{2,1,0:T(8,128)(2,1)}, u32[]{:S(2)}) copy-start(s16[32,136,512]{2,1,0:T(8,128)(2,1)} %copy-done) | copy-start | bytes 13369348

commit v3 on v2

v3 whole, which is shorter than its diff:
```python
import jax
import jax.numpy as jnp
from jax import lax
from jax.experimental import pallas as pl
from jax.experimental.pallas import tpu as pltpu
from jax.sharding import PartitionSpec as P

SLOTS = 14
LANES = 128
EXTRA = 8
BF16, F32 = jnp.bfloat16, jnp.float32
VMEM = pl.BlockSpec(memory_space=pltpu.VMEM)
HBM = pl.BlockSpec(memory_space=pltpu.HBM)


def vmem(mib):
    return pltpu.CompilerParams(vmem_limit_bytes=mib << 20)


def iota(shape, dim):
    return lax.broadcasted_iota(jnp.int32, shape, dim)


def slots_by_row(routes_t, n_expert):
    top, tok = routes_t.shape
    expert = iota((n_expert, tok), 0)
    member = jnp.zeros((n_expert, tok), F32)
    for k in range(top):
        member += jnp.where(routes_t[k : k + 1, :] == expert, 1.0, 0.0)
    earlier = jnp.where(iota((tok, tok), 0) < iota((tok, tok), 1), 1.0, 0.0).astype(BF16)
    slot = jnp.dot(member.astype(BF16), earlier, preferred_element_type=F32)
    slot = jnp.where(member > 0, slot, -1.0).astype(BF16)
    rows = n_expert * SLOTS
    spread = jnp.where(iota((rows, n_expert), 0) // SLOTS == iota((rows, n_expert), 1), 1.0, 0.0).astype(BF16)
    by_row = jnp.dot(spread, slot, preferred_element_type=F32)
    return by_row == (iota((rows, tok), 0) % SLOTS).astype(F32), spread


def pack(rows, wide_ref):
    n = rows.shape[1] // LANES
    for j in range(n):
        wide_ref[pl.ds(j, rows.shape[0], stride=n), :] = rows[:, j * LANES : (j + 1) * LANES]
    return wide_ref[...].astype(BF16)


def unpack(packed, wide_ref, n):
    wide_ref[...] = packed.astype(F32)
    rows = wide_ref.shape[0] // n
    return jnp.concatenate([wide_ref[pl.ds(j, rows, stride=n), :] for j in range(n)], axis=1).astype(BF16)


def dispatch_kernel(routes_ref, latent_ref, out_ref, wide_ref):
    n = latent_ref.shape[1] // LANES
    takes, _ = slots_by_row(routes_ref[...], out_ref.shape[0] // (SLOTS * n))
    rows = jnp.dot(jnp.where(takes, 1.0, 0.0).astype(BF16), latent_ref[...], preferred_element_type=F32)
    out_ref[...] = pack(rows, wide_ref)


def weight_kernel(routes_ref, gates_ref, out_ref):
    n_expert = out_ref.shape[1] // SLOTS
    routes_t, gates_t = routes_ref[...], gates_ref[...].astype(F32)
    takes, spread = slots_by_row(routes_t, n_expert)
    top, tok = routes_t.shape
    expert = iota((n_expert, tok), 0)
    gate = jnp.zeros((n_expert, tok), F32)
    for k in range(top):
        gate += jnp.where(routes_t[k : k + 1, :] == expert, gates_t[k : k + 1, :], 0.0)
    by_row = jnp.dot(spread, gate.astype(BF16), preferred_element_type=F32)
    out_ref[...] = jnp.where(takes, by_row, 0.0).T.astype(BF16)


def expert_kernel(x_ref, in_hbm, out_hbm, out_ref, in_ref, out_w_ref, wide_ref, sems):
    hidden, width = out_w_ref.shape
    step = hidden // sems.shape[0]
    copies = []
    for h in range(0, hidden, step):
        n = h // step
        gate, up = pl.ds(h, step), pl.ds(hidden + h, step)
        copies += [
            pltpu.make_async_copy(in_hbm.at[:, gate], in_ref.at[:, gate], sems.at[n, 0]),
            pltpu.make_async_copy(in_hbm.at[:, up], in_ref.at[:, up], sems.at[n, 1]),
            pltpu.make_async_copy(out_hbm.at[gate, :], out_w_ref.at[gate, :], sems.at[n, 2]),
        ]
    for copy in copies:
        copy.start()
    x = unpack(x_ref[...], wide_ref, width // LANES)
    total = jnp.zeros((x.shape[0], width), F32)
    for copy in copies[:2]:
        copy.wait()
    for h in range(0, hidden, step):
        g = jnp.dot(x, in_ref[:, h : h + step], preferred_element_type=F32)
        u = jnp.dot(x, in_ref[:, hidden + h : hidden + h + step], preferred_element_type=F32)
        if h == 0:
            for copy in copies[2:]:
                copy.wait()
        act = (g / (1.0 + jnp.exp(-g)) * u).astype(BF16)
        total += jnp.dot(act, out_w_ref[h : h + step, :], preferred_element_type=F32)
    out_ref[...] = pack(total, wide_ref)


def power(e):
    return jnp.exp2(e).astype(BF16)


def combine_kernel(w_ref, back_ref, out_ref, wide_ref):
    tok = w_ref.shape[0]
    back = unpack(back_ref[...], wide_ref, out_ref.shape[2] // LANES)
    combined = jnp.dot(w_ref[...], back, preferred_element_type=F32).astype(BF16).astype(F32)
    largest = jnp.maximum(jnp.max(jnp.abs(combined), axis=1, keepdims=True), 2.0**-100)
    e = jnp.floor(jnp.log2(largest) + 1e-4) - 14.0
    whole = jnp.round(combined * power(-e).astype(F32))
    across = jnp.broadcast_to(e, (tok, tok)).T[:EXTRA]
    across = jnp.concatenate([across] * (combined.shape[1] // tok), axis=1)
    out_ref[0] = jnp.concatenate([whole, across]).astype(jnp.int32).astype(jnp.int16)


def part_copy(hbm, ref, sems, i):
    many = ref.shape[0] // sems.shape[0]
    part = pl.ds(i * many, many)
    return pltpu.make_async_copy(hbm.at[part], ref.at[part], sems.at[i])


def rows_and_scales(coded_ref, n, tok):
    coded = coded_ref[n].astype(jnp.int32).astype(F32)
    scale = power(coded[tok : tok + 1, :tok]).astype(F32)
    diagonal = jnp.where(iota((tok, tok), 0) == iota((tok, tok), 1), jnp.broadcast_to(scale, (tok, tok)), 0.0)
    return coded[:tok].astype(BF16), diagonal.astype(BF16)


def grad_kernel(coded_hbm, cot_hbm, out_ref, coded_ref, cot_ref, coded_sems, cot_sems):
    sources, parts = coded_ref.shape[0], coded_sems.shape[0]
    tok = cot_ref.shape[0] // sources
    many = sources // parts
    for i in range(parts):
        part_copy(coded_hbm, coded_ref, coded_sems, i).start()
        part_copy(cot_hbm, cot_ref, cot_sems, i).start()
    total = None
    for i in range(parts):
        part_copy(coded_hbm, coded_ref, coded_sems, i).wait()
        part_copy(cot_hbm, cot_ref, cot_sems, i).wait()
        rows, cots = [], []
        for n in range(i * many, (i + 1) * many):
            coded, diagonal = rows_and_scales(coded_ref, n, tok)
            rows.append(coded)
            cots.append(jnp.dot(diagonal, cot_ref[n * tok : (n + 1) * tok, :], preferred_element_type=F32).astype(BF16))
        part = lax.dot_general(
            jnp.concatenate(cots), jnp.concatenate(rows), (((0,), (0,)), ((), ())), preferred_element_type=F32
        )
        total = part if total is None else total + part
    out_ref[...] = total.T.astype(BF16)


def mixed_kernel(coded_hbm, up_ref, out_hbm, coded_ref, out_ref, coded_sems, out_sems):
    sources, parts = coded_ref.shape[0], coded_sems.shape[0]
    tok = out_ref.shape[0] // sources
    many = sources // parts
    ones = jnp.ones((tok, out_ref.shape[1]), BF16)
    for i in range(parts):
        part_copy(coded_hbm, coded_ref, coded_sems, i).start()
    for i in range(parts):
        part_copy(coded_hbm, coded_ref, coded_sems, i).wait()
        for n in range(i * many, (i + 1) * many):
            coded, diagonal = rows_and_scales(coded_ref, n, tok)
            scale = jnp.dot(diagonal, ones, preferred_element_type=F32)
            mixed = jnp.dot(coded, up_ref[...], preferred_element_type=F32) * scale
            out_ref[n * tok : (n + 1) * tok, :] = mixed.astype(BF16)
        part_copy(out_ref, out_hbm, out_sems, i).start()
    for i in range(parts):
        part_copy(out_ref, out_hbm, out_sems, i).wait()


def body(latent, up_proj, expert_in, expert_out, routes, gates, cotangent):
    n_expert = lax.axis_size("expert")
    n_dp = lax.axis_size("dp")
    tok, width = latent.shape
    cols = up_proj.shape[1]
    slots = n_expert * SLOTS
    sds = jax.ShapeDtypeStruct

    routes_t, gates_t = routes.T, gates.T
    hidden = expert_out.shape[1]
    packed = sds((slots * width // LANES, LANES), BF16)
    wide = pltpu.VMEM(packed.shape, F32)
    per_expert = (n_expert, packed.shape[0] // n_expert, LANES)
    outgoing = pl.pallas_call(
        dispatch_kernel, out_shape=packed, in_specs=[VMEM] * 2, out_specs=VMEM, scratch_shapes=[wide],
        compiler_params=vmem(60), name="dispatch",
    )(routes_t, latent)
    weight = pl.pallas_call(
        weight_kernel, out_shape=sds((tok, slots), BF16), in_specs=[VMEM] * 2, out_specs=VMEM,
        compiler_params=vmem(8), name="weight",
    )(routes_t, gates_t)
    arrived = lax.all_to_all(
        outgoing.reshape(per_expert), "expert", split_axis=0, concat_axis=0, tiled=True
    ).reshape(packed.shape)
    produced = pl.pallas_call(
        expert_kernel, out_shape=packed, in_specs=[VMEM, HBM, HBM], out_specs=VMEM,
        scratch_shapes=[
            pltpu.VMEM((width, 2 * hidden), BF16),
            pltpu.VMEM((hidden, width), BF16),
            wide,
            pltpu.SemaphoreType.DMA((2, 3)),
        ],
        compiler_params=vmem(60), name="expert",
    )(arrived, expert_in[0], expert_out[0])
    back = lax.all_to_all(
        produced.reshape(per_expert), "expert", split_axis=0, concat_axis=0, tiled=True
    ).reshape(packed.shape)
    coded = pl.pallas_call(
        combine_kernel, out_shape=sds((1, tok + EXTRA, width), jnp.int16), in_specs=[VMEM] * 2, out_specs=VMEM,
        scratch_shapes=[wide], compiler_params=vmem(8), name="combine",
    )(weight, back)
    gathered = lax.all_gather(coded, "expert", axis=0, tiled=True)
    parts = n_expert // 8
    coded_parts = [pltpu.VMEM(gathered.shape, gathered.dtype)]
    sems = [pltpu.SemaphoreType.DMA((parts,))] * 2
    whole = [pltpu.VMEM(cotangent.shape, BF16)]
    grad = pl.pallas_call(
        grad_kernel, out_shape=sds((width, cols), BF16), in_specs=[HBM, HBM], out_specs=VMEM,
        scratch_shapes=coded_parts + whole + sems, compiler_params=vmem(60), name="grad",
    )(gathered, cotangent)
    mixed = pl.pallas_call(
        mixed_kernel, out_shape=sds(cotangent.shape, BF16), in_specs=[HBM, VMEM], out_specs=HBM,
        scratch_shapes=coded_parts + whole + sems, compiler_params=vmem(60), name="mixed",
        cost_estimate=pl.CostEstimate(flops=2 * cotangent.shape[0] * width * cols, bytes_accessed=6 << 20, transcendentals=0),
    )(gathered, up_proj)

    parts = lax.all_to_all(grad.reshape(n_dp, width // n_dp, cols), "dp", split_axis=0, concat_axis=0, tiled=True)
    parts, mixed = lax.optimization_barrier((parts, mixed))
    mine = jnp.sum(parts.astype(F32), axis=0).astype(BF16)
    spread = jnp.broadcast_to(mine[None], (n_dp,) + mine.shape)
    grad_up = lax.all_to_all(spread, "dp", split_axis=0, concat_axis=0, tiled=True).astype(F32)
    return mixed, grad_up.reshape(width, cols)


def solution(mesh):
    in_specs = (
        P(("dp", "expert"), None),
        P(None, "expert"),
        P("expert", None, None),
        P("expert", None, None),
        P(("dp", "expert"), None),
        P(("dp", "expert"), None),
        P("dp", "expert"),
    )
    out_specs = (P("dp", "expert"), P(None, "expert"))
    return jax.shard_map(body, mesh=mesh, in_specs=in_specs, out_specs=out_specs, check_vma=False)
```

time: 192 us -> 180 us (0.938)
  local copies, waits for them, and re-layouts: 8.19 us -> 0.03 us
  blocking collectives: 118 us -> 110 us
  starting transfers between devices: 8.04 us -> 13.8 us
    all_to_all x2, blocking collectives: 73.2 us -> 64.8 us  [the longest x1 51.3 us: body(): lax.all_to_all(outgoing.reshape(per_expert), 'expert', split_axis=0, conc...]
    unnamed x13 -> x4, local copies, waits for them, and re-layouts: 7.47 us -> 0.01 us
    all_to_all x2, starting transfers between devices: 8.04 us -> 13.8 us  [the longest x1 9.72 us: body(): lax.all_to_all(grad.reshape(n_dp, width // n_dp, cols), 'dp', split_axis=...]
where the time goes in v3:
time: 180 us; the launch traced here: 179 us
  blocking collectives  110 us (61%)
  waiting for transfers between devices  35.2 us (20%)
  Pallas kernels  18.8 us (10%)
  starting transfers between devices  13.8 us (8%)
    all_to_all x1, blocking collectives, body(): lax.all_to_all(outgoing.reshape(per_expert), 'expert', split_axis=0, conc...  51.3 us
    all_gather x1, blocking collectives, body(): gathered = lax.all_gather(coded, 'expert', axis=0, tiled=True)  45.3 us
    all_to_all x1, waiting for transfers between devices, body(): lax.all_to_all(produced.reshape(per_expert), 'expert', split_axis=0, conc...  30.3 us
    all_to_all x1, blocking collectives, body(): lax.all_to_all(spread, 'dp', split_axis=0, concat_axis=0, tiled=True)  13.5 us
    all_to_all x1, starting transfers between devices, body(): lax.all_to_all(grad.reshape(n_dp, width // n_dp, cols), 'dp', split_axis=...  9.72 us
    pallas_call x1, Pallas kernels, body(): pl.pallas_call(expert_kernel, out_shape=packed, in_specs=[VMEM, HBM, HBM]...  6.91 us
    pallas_call x1, Pallas kernels, body(): pl.pallas_call(mixed_kernel, out_shape=sds(cotangent.shape, BF16), in_spe...  4.93 us
    all_to_all x1, waiting for transfers between devices, body(): lax.all_to_all(grad.reshape(n_dp, width // n_dp, cols), 'dp', split_axis=...  4.89 us
  transfers between devices with their start and end apart: 2, of which 2 were waited for; matrix products, arithmetic and copies ran while one was open for 0% of the time, Pallas kernels for 3%

profile of v3, /device:TPU:1, one launch (start us, length us, event | category | flops | bytes accessed | tf_op | source)
XLA Modules:
  0.0 179.4 jit_solution(14750343727471367584)
XLA Ops:
  0.6 2.3 %dispatch.1 = bf16[1792,128]{1,0:T(8,128)(2,1)} custom-call(s32[8,128]{1,0:T(8,128)} %bitcast.13, bf16[128,512]{1,0:T(8,128)(2,1)} %latent_ref.1), custom_call_target="tpu_custom_call" | custom-call | tf_op jit(solution)/shard_map/dispatch/pallas_call | solution.py:185
  2.9 51.3 %all_to_all.20 = bf16[32,56,128]{2,1,0:T(8,128)(2,1)} all-to-all(bf16[32,56,128]{2,1,0:T(8,128)(2,1)} %bitcast.20), channel_id=1, replica_groups=mesh['dp'=32,'expert'=32] {'expert'}, dimensions={0} | all-to-all | bytes 917504 | tf_op jit(solution)/shard_map/all_to_all | solution.py:193
  54.2 0.0 copy-start
  54.2 0.0 copy-start.1
  54.2 6.9 %expert.1 = bf16[1792,128]{1,0:T(8,128)(2,1)} custom-call(bf16[1792,128]{1,0:T(8,128)(2,1)} %bitcast.19, bf16[512,4096]{1,0:T(8,128)(2,1)} %bitcast.16, bf16[2048,512]{1,0:T(8,128)(2,1)} %bitcast.17), custom_call_target="tpu_custom_call" | custom-call | tf_op jit(solution)/shard_map/expert/pallas_call | solution.py:196
  61.1 4.0 %all-to-all-start.1 = ((bf16[32,56,128]{2,1,0:T(8,128)(2,1)}), bf16[32,56,128]{2,1,0:T(8,128)(2,1)S(1)}, u32[]{:S(2)}, u32[]{:S(2)}) async-start(bf16[32,56,128]{2,1,0:T(8,128)(2,1)} %bitcast.18), calls=%async_computation.1 | async-start | bytes 917504 | tf_op jit(solution)/shard_map/all_to_all | solution.py:206
  65.1 0.0 copy-done
  65.1 0.0 copy-done.1
  65.1 0.4 weight.1.w_ref
  65.6 30.3 %all-to-all-done.1 = bf16[32,56,128]{2,1,0:T(8,128)(2,1)S(1)} async-done(((bf16[32,56,128]{2,1,0:T(8,128)(2,1)}), bf16[32,56,128]{2,1,0:T(8,128)(2,1)S(1)}, u32[]{:S(2)}, u32[]{:S(2)}) %all-to-all-start.1) | async-done | bytes 458784 | tf_op jit(solution)/shard_map/all_to_all | solution.py:206
  95.9 0.4 combine.1
  96.3 45.3 %all-gather.1.coded_hbm = s16[32,136,512]{2,1,0:T(8,128)(2,1)} all-gather(s16[1,136,512]{2,1,0:T(8,128)(2,1)S(1)} %combine.1), channel_id=1, replica_groups=mesh['dp'=32,'expert'=32] {'expert'}, dimensions={0}, use_global_device_ids=true | all-gather | bytes 4595712 | tf_op jit(solution)/shard_map/all_gather | solution.py:213
  141.6 3.9 %grad.1 = bf16[512,128]{1,0:T(8,128)(2,1)} custom-call(s16[32,136,512]{2,1,0:T(8,128)(2,1)} %all-gather.1.coded_hbm, bf16[4096,128]{1,0:T(8,128)(2,1)} %cot_hbm.1), custom_call_target="tpu_custom_call" | custom-call | tf_op jit(solution)/shard_map/grad/pallas_call | solution.py:218
  145.5 9.7 %all-to-all-start.2 = ((bf16[32,16,128]{2,1,0:T(8,128)(2,1)}), bf16[32,16,128]{2,1,0:T(8,128)(2,1)S(1)}, u32[]{:S(2)}, u32[]{:S(2)}) async-start(bf16[32,16,128]{2,1,0:T(8,128)(2,1)} %bitcast.21), calls=%async_computation.2 | async-start | bytes 262144 | tf_op jit(solution)/shard_map/all_to_all | solution.py:228
  155.2 4.9 %mixed.1 = bf16[4096,128]{1,0:T(8,128)(2,1)} custom-call(s16[32,136,512]{2,1,0:T(8,128)(2,1)} %all-gather.1.coded_hbm, bf16[512,128]{1,0:T(8,128)(2,1)} %up_ref.1), custom_call_target="tpu_custom_call" | custom-call | flops 536870912 | bytes 6291456 | tf_op jit(solution)/shard_map/mixed/pallas_call | solution.py:222
  160.2 4.9 %all-to-all-done.2 = bf16[32,16,128]{2,1,0:T(8,128)(2,1)S(1)} async-done(((bf16[32,16,128]{2,1,0:T(8,128)(2,1)}), bf16[32,16,128]{2,1,0:T(8,128)(2,1)S(1)}, u32[]{:S(2)}, u32[]{:S(2)}) %all-to-all-start.2) | async-done | bytes 131104 | tf_op jit(solution)/shard_map/all_to_all | solution.py:228
  165.1 13.5 %all_to_all.21 = bf16[32,16,128]{2,1,0:T(8,128)(2,1)S(1)} all-to-all(bf16[32,16,128]{2,1,0:T(8,128)(2,1)S(1)} %broadcast_in_dim.2), channel_id=1, replica_groups=mesh['dp'=32,'expert'=32] {'dp'}, dimensions={0} | all-to-all | bytes 262144 | tf_op jit(solution)/shard_map/all_to_all | solution.py:232
  178.6 0.7 bitcast_convert_fusion
  (2 shorter events, 0.1 us)
Async XLA Ops:
  54.2 11.0 %copy-start = (s32[128,8]{0,1:T(8,128)S(1)}, s32[128,8]{0,1:T(8,128)}, u32[]{:S(2)}) copy-start(s32[128,8]{0,1:T(8,128)} %param.11) | copy-start | bytes 12292
  54.2 11.0 %copy-start.1 = (bf16[128,8]{0,1:T(8,128)(2,1)S(1)}, bf16[128,8]{0,1:T(8,128)(2,1)}, u32[]{:S(2)}) copy-start(bf16[128,8]{0,1:T(8,128)(2,1)} %param.12) | copy-start | bytes 6148
  61.1 34.8 %all-to-all-start.1 = ((bf16[32,56,128]{2,1,0:T(8,128)(2,1)}), bf16[32,56,128]{2,1,0:T(8,128)(2,1)S(1)}, u32[]{:S(2)}, u32[]{:S(2)}) async-start(bf16[32,56,128]{2,1,0:T(8,128)(2,1)} %bitcast.18), calls=%async_computation.1 | async-start | bytes 917504 | tf_op jit(solution)/shard_map/all_to_all | solution.py:206
  145.5 19.6 %all-to-all-start.2 = ((bf16[32,16,128]{2,1,0:T(8,128)(2,1)}), bf16[32,16,128]{2,1,0:T(8,128)(2,1)S(1)}, u32[]{:S(2)}, u32[]{:S(2)}) async-start(bf16[32,16,128]{2,1,0:T(8,128)(2,1)} %bitcast.21), calls=%async_computation.2 | async-start | bytes 262144 | tf_op jit(solution)/shard_map/all_to_all | solution.py:228

commit v4 on v3

--- a/solution.py
+++ b/solution.py
@@ -5,7 +5,7 @@
 from jax.experimental.pallas import tpu as pltpu
 from jax.sharding import PartitionSpec as P
 
-SLOTS = 14
+SLOTS = 13
 LANES = 128
 EXTRA = 8
 BF16, F32 = jnp.bfloat16, jnp.float32
@@ -69,30 +69,14 @@
     out_ref[...] = jnp.where(takes, by_row, 0.0).T.astype(BF16)
 
 
-def expert_kernel(x_ref, in_hbm, out_hbm, out_ref, in_ref, out_w_ref, wide_ref, sems):
+def expert_kernel(x_ref, in_ref, out_w_ref, out_ref, wide_ref):
     hidden, width = out_w_ref.shape
-    step = hidden // sems.shape[0]
-    copies = []
-    for h in range(0, hidden, step):
-        n = h // step
-        gate, up = pl.ds(h, step), pl.ds(hidden + h, step)
-        copies += [
-            pltpu.make_async_copy(in_hbm.at[:, gate], in_ref.at[:, gate], sems.at[n, 0]),
-            pltpu.make_async_copy(in_hbm.at[:, up], in_ref.at[:, up], sems.at[n, 1]),
-            pltpu.make_async_copy(out_hbm.at[gate, :], out_w_ref.at[gate, :], sems.at[n, 2]),
-        ]
-    for copy in copies:
-        copy.start()
+    step = 512
     x = unpack(x_ref[...], wide_ref, width // LANES)
     total = jnp.zeros((x.shape[0], width), F32)
-    for copy in copies[:2]:
-        copy.wait()
     for h in range(0, hidden, step):
         g = jnp.dot(x, in_ref[:, h : h + step], preferred_element_type=F32)
         u = jnp.dot(x, in_ref[:, hidden + h : hidden + h + step], preferred_element_type=F32)
-        if h == 0:
-            for copy in copies[2:]:
-                copy.wait()
         act = (g / (1.0 + jnp.exp(-g)) * u).astype(BF16)
         total += jnp.dot(act, out_w_ref[h : h + step, :], preferred_element_type=F32)
     out_ref[...] = pack(total, wide_ref)
@@ -181,10 +165,11 @@
     hidden = expert_out.shape[1]
     packed = sds((slots * width // LANES, LANES), BF16)
     wide = pltpu.VMEM(packed.shape, F32)
-    per_expert = (n_expert, packed.shape[0] // n_expert, LANES)
+    per_expert = (n_expert, SLOTS, width // LANES, LANES)
     outgoing = pl.pallas_call(
         dispatch_kernel, out_shape=packed, in_specs=[VMEM] * 2, out_specs=VMEM, scratch_shapes=[wide],
-        compiler_params=vmem(60), name="dispatch",
+        compiler_params=vmem(8), name="dispatch",
+        cost_estimate=pl.CostEstimate(flops=6000000000, bytes_accessed=10000000, transcendentals=0),
     )(routes_t, latent)
     weight = pl.pallas_call(
         weight_kernel, out_shape=sds((tok, slots), BF16), in_specs=[VMEM] * 2, out_specs=VMEM,
@@ -194,14 +179,8 @@
         outgoing.reshape(per_expert), "expert", split_axis=0, concat_axis=0, tiled=True
     ).reshape(packed.shape)
     produced = pl.pallas_call(
-        expert_kernel, out_shape=packed, in_specs=[VMEM, HBM, HBM], out_specs=VMEM,
-        scratch_shapes=[
-            pltpu.VMEM((width, 2 * hidden), BF16),
-            pltpu.VMEM((hidden, width), BF16),
-            wide,
-            pltpu.SemaphoreType.DMA((2, 3)),
-        ],
-        compiler_params=vmem(60), name="expert",
+        expert_kernel, out_shape=packed, in_specs=[VMEM] * 3, out_specs=VMEM, scratch_shapes=[wide],
+        compiler_params=vmem(20), name="expert",
     )(arrived, expert_in[0], expert_out[0])
     back = lax.all_to_all(
         produced.reshape(per_expert), "expert", split_axis=0, concat_axis=0, tiled=True

time: 180 us -> 174 us (0.967)
  Pallas kernels: 18.8 us -> 14 us
    pallas_call x1, Pallas kernels: 6.91 us -> 3.76 us  [body(): pl.pallas_call(expert_kernel, out_shape=packed, in_specs=[VMEM] * 3, out_...]
where the time goes in v4:
time: 174 us; the launch traced here: 173 us
  blocking collectives  109 us (63%)
  waiting for transfers between devices  33.7 us (19%)
  Pallas kernels  14 us (8%)
  starting transfers between devices  13.8 us (8%)
    all_to_all x1, blocking collectives, body(): lax.all_to_all(outgoing.reshape(per_expert), 'expert', split_axis=0, conc...  49.8 us
    all_gather x1, blocking collectives, body(): gathered = lax.all_gather(coded, 'expert', axis=0, tiled=True)  45.5 us
    all_to_all x1, waiting for transfers between devices, body(): lax.all_to_all(produced.reshape(per_expert), 'expert', split_axis=0, conc...  28.9 us
    all_to_all x1, blocking collectives, body(): lax.all_to_all(spread, 'dp', split_axis=0, concat_axis=0, tiled=True)  13.5 us
    all_to_all x1, starting transfers between devices, body(): lax.all_to_all(grad.reshape(n_dp, width // n_dp, cols), 'dp', split_axis=...  9.69 us
    pallas_call x1, Pallas kernels, body(): pl.pallas_call(mixed_kernel, out_shape=sds(cotangent.shape, BF16), in_spe...  4.93 us
    all_to_all x1, waiting for transfers between devices, body(): lax.all_to_all(grad.reshape(n_dp, width // n_dp, cols), 'dp', split_axis=...  4.89 us
    all_to_all x1, starting transfers between devices, body(): lax.all_to_all(produced.reshape(per_expert), 'expert', split_axis=0, conc...  4.12 us
  transfers between devices with their start and end apart: 2, of which 2 were waited for; matrix products, arithmetic and copies ran while one was open for 0% of the time, Pallas kernels for 3%

profile of v4, /device:TPU:1, one launch (start us, length us, event | category | flops | bytes accessed | tf_op | source)
XLA Modules:
  0.0 173.4 jit_solution(629203052402938208)
XLA Ops:
  0.6 0.0 copy-start.2
  0.6 0.7 copy-done.2
  1.3 0.0 copy-start.5
  1.3 0.9 copy-done.5
  2.2 0.0 copy-start
  2.2 0.0 copy-start.1
  2.2 0.6 dispatch.1
  2.8 49.8 %all_to_all.20 = bf16[32,13,4,128]{3,2,1,0:T(4,128)(2,1)S(1)} all-to-all(bf16[32,13,4,128]{3,2,1,0:T(4,128)(2,1)S(1)} %bitcast.16), channel_id=1, replica_groups=mesh['dp'=32,'expert'=32] {'expert'}, dimensions={0} | all-to-all | bytes 851968 | tf_op jit(solution)/shard_map/all_to_all | solution.py:178
  52.5 0.0 copy-start.3
  52.5 0.0 copy-start.4
  52.5 0.0 copy-done
  52.5 0.0 copy-done.1
  52.6 3.8 %expert.1 = bf16[1664,128]{1,0:T(8,128)(2,1)} custom-call(bf16[1664,128]{1,0:T(8,128)(2,1)S(1)} %bitcast.14, bf16[512,4096]{1,0:T(8,128)(2,1)S(1)} %bitcast.12, bf16[2048,512]{1,0:T(8,128)(2,1)S(1)} %bitcast.13), custom_call_target="tpu_custom_call" | custom-call | tf_op jit(solution)/shard_map/expert/pallas_call | solution.py:181
  56.3 4.1 %all-to-all-start.1 = ((bf16[32,13,4,128]{3,2,1,0:T(4,128)(2,1)}), bf16[32,13,4,128]{3,2,1,0:T(4,128)(2,1)S(1)}, u32[]{:S(2)}, u32[]{:S(2)}) async-start(bf16[32,13,4,128]{3,2,1,0:T(4,128)(2,1)} %bitcast.6), calls=%async_computation.1 | async-start | bytes 851968 | tf_op jit(solution)/shard_map/all_to_all | solution.py:185
  60.4 0.0 copy-done.3
  60.5 0.0 copy-done.4
  60.5 0.4 weight.1.w_ref
  60.9 28.9 %all-to-all-done.1 = bf16[32,13,4,128]{3,2,1,0:T(4,128)(2,1)S(1)} async-done(((bf16[32,13,4,128]{3,2,1,0:T(4,128)(2,1)}), bf16[32,13,4,128]{3,2,1,0:T(4,128)(2,1)S(1)}, u32[]{:S(2)}, u32[]{:S(2)}) %all-to-all-start.1) | async-done | bytes 426016 | tf_op jit(solution)/shard_map/all_to_all | solution.py:185
  89.7 0.4 combine.1
  90.2 45.5 %all-gather.1.coded_hbm = s16[32,136,512]{2,1,0:T(8,128)(2,1)} all-gather(s16[1,136,512]{2,1,0:T(8,128)(2,1)S(1)} %combine.1), channel_id=1, replica_groups=mesh['dp'=32,'expert'=32] {'expert'}, dimensions={0}, use_global_device_ids=true | all-gather | bytes 4595712 | tf_op jit(solution)/shard_map/all_gather | solution.py:192
  135.7 3.9 %grad.1 = bf16[512,128]{1,0:T(8,128)(2,1)} custom-call(s16[32,136,512]{2,1,0:T(8,128)(2,1)} %all-gather.1.coded_hbm, bf16[4096,128]{1,0:T(8,128)(2,1)} %cot_hbm.1), custom_call_target="tpu_custom_call" | custom-call | tf_op jit(solution)/shard_map/grad/pallas_call | solution.py:197
  139.6 9.7 %all-to-all-start.2 = ((bf16[32,16,128]{2,1,0:T(8,128)(2,1)}), bf16[32,16,128]{2,1,0:T(8,128)(2,1)S(1)}, u32[]{:S(2)}, u32[]{:S(2)}) async-start(bf16[32,16,128]{2,1,0:T(8,128)(2,1)} %bitcast.20), calls=%async_computation.2 | async-start | bytes 262144 | tf_op jit(solution)/shard_map/all_to_all | solution.py:207
  149.3 4.9 %mixed.1 = bf16[4096,128]{1,0:T(8,128)(2,1)} custom-call(s16[32,136,512]{2,1,0:T(8,128)(2,1)} %all-gather.1.coded_hbm, bf16[512,128]{1,0:T(8,128)(2,1)} %up_ref.1), custom_call_target="tpu_custom_call" | custom-call | flops 536870912 | bytes 6291456 | tf_op jit(solution)/shard_map/mixed/pallas_call | solution.py:201
  154.2 4.9 %all-to-all-done.2 = bf16[32,16,128]{2,1,0:T(8,128)(2,1)S(1)} async-done(((bf16[32,16,128]{2,1,0:T(8,128)(2,1)}), bf16[32,16,128]{2,1,0:T(8,128)(2,1)S(1)}, u32[]{:S(2)}, u32[]{:S(2)}) %all-to-all-start.2) | async-done | bytes 131104 | tf_op jit(solution)/shard_map/all_to_all | solution.py:207
  159.2 13.5 %all_to_all.21 = bf16[32,16,128]{2,1,0:T(8,128)(2,1)S(1)} all-to-all(bf16[32,16,128]{2,1,0:T(8,128)(2,1)S(1)} %broadcast_in_dim.2), channel_id=1, replica_groups=mesh['dp'=32,'expert'=32] {'dp'}, dimensions={0} | all-to-all | bytes 262144 | tf_op jit(solution)/shard_map/all_to_all | solution.py:211
  172.6 0.7 bitcast_convert_fusion
  (2 shorter events, 0.1 us)
Async XLA Ops:
  0.6 0.7 copy-start.2
  1.3 0.9 copy-start.5
  2.2 50.3 %copy-start = (bf16[1,512,4096]{2,1,0:T(8,128)(2,1)S(1)}, bf16[1,512,4096]{2,1,0:T(8,128)(2,1)}, u32[]{:S(2)}) copy-start(bf16[1,512,4096]{2,1,0:T(8,128)(2,1)} %param.9) | copy-start | bytes 12582916
  2.2 50.3 %copy-start.1 = (bf16[1,2048,512]{2,1,0:T(8,128)(2,1)S(1)}, bf16[1,2048,512]{2,1,0:T(8,128)(2,1)}, u32[]{:S(2)}) copy-start(bf16[1,2048,512]{2,1,0:T(8,128)(2,1)} %param.10) | copy-start | bytes 6291460
  52.5 7.9 %copy-start.3 = (s32[128,8]{0,1:T(8,128)S(1)}, s32[128,8]{0,1:T(8,128)}, u32[]{:S(2)}) copy-start(s32[128,8]{0,1:T(8,128)} %param.11) | copy-start | bytes 12292
  52.5 7.9 %copy-start.4 = (bf16[128,8]{0,1:T(8,128)(2,1)S(1)}, bf16[128,8]{0,1:T(8,128)(2,1)}, u32[]{:S(2)}) copy-start(bf16[128,8]{0,1:T(8,128)(2,1)} %param.12) | copy-start | bytes 6148
  56.3 33.4 %all-to-all-start.1 = ((bf16[32,13,4,128]{3,2,1,0:T(4,128)(2,1)}), bf16[32,13,4,128]{3,2,1,0:T(4,128)(2,1)S(1)}, u32[]{:S(2)}, u32[]{:S(2)}) async-start(bf16[32,13,4,128]{3,2,1,0:T(4,128)(2,1)} %bitcast.6), calls=%async_computation.1 | async-start | bytes 851968 | tf_op jit(solution)/shard_map/all_to_all | solution.py:185
  139.6 19.5 %all-to-all-start.2 = ((bf16[32,16,128]{2,1,0:T(8,128)(2,1)}), bf16[32,16,128]{2,1,0:T(8,128)(2,1)S(1)}, u32[]{:S(2)}, u32[]{:S(2)}) async-start(bf16[32,16,128]{2,1,0:T(8,128)(2,1)} %bitcast.20), calls=%async_computation.2 | async-start | bytes 262144 | tf_op jit(solution)/shard_map/all_to_all | solution.py:207

commit v5 on v4

--- a/solution.py
+++ b/solution.py
@@ -111,16 +111,16 @@
     return coded[:tok].astype(BF16), diagonal.astype(BF16)
 
 
-def grad_kernel(coded_hbm, cot_hbm, out_ref, coded_ref, cot_ref, coded_sems, cot_sems):
-    sources, parts = coded_ref.shape[0], coded_sems.shape[0]
+def grad_kernel(coded_ref, cot_hbm, out_ref, coded_hbm, cot_ref, coded_sem, cot_sems):
+    sources, parts = coded_ref.shape[0], cot_sems.shape[0]
     tok = cot_ref.shape[0] // sources
     many = sources // parts
     for i in range(parts):
-        part_copy(coded_hbm, coded_ref, coded_sems, i).start()
         part_copy(cot_hbm, cot_ref, cot_sems, i).start()
+    keep = pltpu.make_async_copy(coded_ref, coded_hbm.at[pl.ds(0, sources)], coded_sem)
+    keep.start()
     total = None
     for i in range(parts):
-        part_copy(coded_hbm, coded_ref, coded_sems, i).wait()
         part_copy(cot_hbm, cot_ref, cot_sems, i).wait()
         rows, cots = [], []
         for n in range(i * many, (i + 1) * many):
@@ -132,6 +132,7 @@
         )
         total = part if total is None else total + part
     out_ref[...] = total.T.astype(BF16)
+    keep.wait()
 
 
 def mixed_kernel(coded_hbm, up_ref, out_hbm, coded_ref, out_ref, coded_sems, out_sems):
@@ -194,15 +195,17 @@
     coded_parts = [pltpu.VMEM(gathered.shape, gathered.dtype)]
     sems = [pltpu.SemaphoreType.DMA((parts,))] * 2
     whole = [pltpu.VMEM(cotangent.shape, BF16)]
-    grad = pl.pallas_call(
-        grad_kernel, out_shape=sds((width, cols), BF16), in_specs=[HBM, HBM], out_specs=VMEM,
-        scratch_shapes=coded_parts + whole + sems, compiler_params=vmem(60), name="grad",
+    room = sds((2 * n_expert,) + gathered.shape[1:], gathered.dtype)
+    grad, kept = pl.pallas_call(
+        grad_kernel, out_shape=[sds((width, cols), BF16), room],
+        in_specs=[VMEM, HBM], out_specs=[VMEM, HBM],
+        scratch_shapes=whole + [pltpu.SemaphoreType.DMA, sems[0]], compiler_params=vmem(47), name="grad",
     )(gathered, cotangent)
     mixed = pl.pallas_call(
         mixed_kernel, out_shape=sds(cotangent.shape, BF16), in_specs=[HBM, VMEM], out_specs=HBM,
         scratch_shapes=coded_parts + whole + sems, compiler_params=vmem(60), name="mixed",
         cost_estimate=pl.CostEstimate(flops=2 * cotangent.shape[0] * width * cols, bytes_accessed=6 << 20, transcendentals=0),
-    )(gathered, up_proj)
+    )(kept, up_proj)
 
     parts = lax.all_to_all(grad.reshape(n_dp, width // n_dp, cols), "dp", split_axis=0, concat_axis=0, tiled=True)
     parts, mixed = lax.optimization_barrier((parts, mixed))

time: 174 us -> 172 us (0.989)
  no operation moved by 1% of the time
where the time goes in v5:
time: 172 us; the launch traced here: 171 us
  blocking collectives  108 us (63%)
  waiting for transfers between devices  33.7 us (20%)
  starting transfers between devices  13.9 us (8%)
  Pallas kernels  12.9 us (8%)
    all_to_all x1, blocking collectives, body(): lax.all_to_all(outgoing.reshape(per_expert), 'expert', split_axis=0, conc...  49.8 us
    all_gather x1, blocking collectives, body(): gathered = lax.all_gather(coded, 'expert', axis=0, tiled=True)  44.4 us
    all_to_all x1, waiting for transfers between devices, body(): lax.all_to_all(produced.reshape(per_expert), 'expert', split_axis=0, conc...  28.9 us
    all_to_all x1, blocking collectives, body(): lax.all_to_all(spread, 'dp', split_axis=0, concat_axis=0, tiled=True)  13.5 us
    all_to_all x1, starting transfers between devices, body(): lax.all_to_all(grad.reshape(n_dp, width // n_dp, cols), 'dp', split_axis=...  9.69 us
    pallas_call x1, Pallas kernels, body(): pl.pallas_call(mixed_kernel, out_shape=sds(cotangent.shape, BF16), in_spe...  4.93 us
    all_to_all x1, waiting for transfers between devices, body(): lax.all_to_all(grad.reshape(n_dp, width // n_dp, cols), 'dp', split_axis=...  4.89 us
    all_to_all x1, starting transfers between devices, body(): lax.all_to_all(produced.reshape(per_expert), 'expert', split_axis=0, conc...  4.25 us
  transfers between devices with their start and end apart: 2, of which 2 were waited for; matrix products, arithmetic and copies ran while one was open for 0% of the time, Pallas kernels for 3%

profile of v5, /device:TPU:1, one launch (start us, length us, event | category | flops | bytes accessed | tf_op | source)
XLA Modules:
  0.0 171.3 jit_solution(16922400290373869278)
XLA Ops:
  0.6 0.0 copy-start.3
  0.6 0.7 copy-done.3
  1.3 0.0 copy-start.6
  1.3 0.9 copy-done.6
  2.2 0.0 copy-start
  2.2 0.0 copy-start.1
  2.2 0.6 dispatch.1
  2.8 0.0 copy-start.4
  2.8 0.0 copy-start.5
  2.8 49.8 %all_to_all.20 = bf16[32,13,4,128]{3,2,1,0:T(4,128)(2,1)S(1)} all-to-all(bf16[32,13,4,128]{3,2,1,0:T(4,128)(2,1)S(1)} %bitcast.16), channel_id=1, replica_groups=mesh['dp'=32,'expert'=32] {'expert'}, dimensions={0} | all-to-all | bytes 851968 | tf_op jit(solution)/shard_map/all_to_all | solution.py:179
  52.6 0.0 copy-done
  52.6 0.0 copy-done.1
  52.6 3.8 %expert.1 = bf16[1664,128]{1,0:T(8,128)(2,1)} custom-call(bf16[1664,128]{1,0:T(8,128)(2,1)S(1)} %bitcast.14, bf16[512,4096]{1,0:T(8,128)(2,1)S(1)} %bitcast.12, bf16[2048,512]{1,0:T(8,128)(2,1)S(1)} %bitcast.13), custom_call_target="tpu_custom_call" | custom-call | tf_op jit(solution)/shard_map/expert/pallas_call | solution.py:182
  56.3 0.0 copy-start.2
  56.3 4.2 %all-to-all-start.1 = ((bf16[32,13,4,128]{3,2,1,0:T(4,128)(2,1)}), bf16[32,13,4,128]{3,2,1,0:T(4,128)(2,1)S(1)}, u32[]{:S(2)}, u32[]{:S(2)}) async-start(bf16[32,13,4,128]{3,2,1,0:T(4,128)(2,1)} %bitcast.6), calls=%async_computation.1 | async-start | bytes 851968 | tf_op jit(solution)/shard_map/all_to_all | solution.py:186
  60.6 0.0 copy-done.4
  60.6 0.0 copy-done.5
  60.6 0.4 weight.1.w_ref
  61.0 28.9 %all-to-all-done.1 = bf16[32,13,4,128]{3,2,1,0:T(4,128)(2,1)S(1)} async-done(((bf16[32,13,4,128]{3,2,1,0:T(4,128)(2,1)}), bf16[32,13,4,128]{3,2,1,0:T(4,128)(2,1)S(1)}, u32[]{:S(2)}, u32[]{:S(2)}) %all-to-all-start.1) | async-done | bytes 426016 | tf_op jit(solution)/shard_map/all_to_all | solution.py:186
  89.9 0.4 combine.1
  90.3 44.4 %all-gather.1.coded_ref = s16[32,136,512]{2,1,0:T(8,128)(2,1)S(1)} all-gather(s16[1,136,512]{2,1,0:T(8,128)(2,1)S(1)} %combine.1), channel_id=1, replica_groups=mesh['dp'=32,'expert'=32] {'expert'}, dimensions={0}, use_global_device_ids=true | all-gather | bytes 4595712 | tf_op jit(solution)/shard_map/all_gather | solution.py:193
  134.7 0.0 copy-done.2
  134.7 2.8 %grad.1 = (bf16[512,128]{1,0:T(8,128)(2,1)}, s16[64,136,512]{2,1,0:T(8,128)(2,1)}) custom-call(s16[32,136,512]{2,1,0:T(8,128)(2,1)S(1)} %all-gather.1.coded_ref, bf16[4096,128]{1,0:T(8,128)(2,1)S(1)} %copy-done.2), custom_call_target="tpu_custom_call" | custom-call | tf_op jit(solution)/shard_map/grad/pallas_call | solution.py:199
  137.5 9.7 %all-to-all-start.2 = ((bf16[32,16,128]{2,1,0:T(8,128)(2,1)}), bf16[32,16,128]{2,1,0:T(8,128)(2,1)S(1)}, u32[]{:S(2)}, u32[]{:S(2)}) async-start(bf16[32,16,128]{2,1,0:T(8,128)(2,1)} %bitcast.8), calls=%async_computation.2 | async-start | bytes 262144 | tf_op jit(solution)/shard_map/all_to_all | solution.py:210
  147.2 4.9 %mixed.1 = bf16[4096,128]{1,0:T(8,128)(2,1)} custom-call(s16[64,136,512]{2,1,0:T(8,128)(2,1)} %get-tuple-element.7.coded_hbm, bf16[512,128]{1,0:T(8,128)(2,1)} %up_ref.1), custom_call_target="tpu_custom_call" | custom-call | flops 536870912 | bytes 6291456 | tf_op jit(solution)/shard_map/mixed/pallas_call | solution.py:204
  152.1 4.9 %all-to-all-done.2 = bf16[32,16,128]{2,1,0:T(8,128)(2,1)S(1)} async-done(((bf16[32,16,128]{2,1,0:T(8,128)(2,1)}), bf16[32,16,128]{2,1,0:T(8,128)(2,1)S(1)}, u32[]{:S(2)}, u32[]{:S(2)}) %all-to-all-start.2) | async-done | bytes 131104 | tf_op jit(solution)/shard_map/all_to_all | solution.py:210
  157.1 13.5 %all_to_all.21 = bf16[32,16,128]{2,1,0:T(8,128)(2,1)S(1)} all-to-all(bf16[32,16,128]{2,1,0:T(8,128)(2,1)S(1)} %broadcast_in_dim.2), channel_id=1, replica_groups=mesh['dp'=32,'expert'=32] {'dp'}, dimensions={0} | all-to-all | bytes 262144 | tf_op jit(solution)/shard_map/all_to_all | solution.py:214
  170.6 0.7 bitcast_convert_fusion
  (2 shorter events, 0.1 us)
Async XLA Ops:
  0.6 0.7 copy-start.3
  1.3 0.9 copy-start.6
  2.2 50.3 %copy-start = (bf16[1,512,4096]{2,1,0:T(8,128)(2,1)S(1)}, bf16[1,512,4096]{2,1,0:T(8,128)(2,1)}, u32[]{:S(2)}) copy-start(bf16[1,512,4096]{2,1,0:T(8,128)(2,1)} %param.9) | copy-start | bytes 12582916
  2.2 50.3 %copy-start.1 = (bf16[1,2048,512]{2,1,0:T(8,128)(2,1)S(1)}, bf16[1,2048,512]{2,1,0:T(8,128)(2,1)}, u32[]{:S(2)}) copy-start(bf16[1,2048,512]{2,1,0:T(8,128)(2,1)} %param.10) | copy-start | bytes 6291460
  2.8 57.8 %copy-start.4 = (s32[128,8]{0,1:T(8,128)S(1)}, s32[128,8]{0,1:T(8,128)}, u32[]{:S(2)}) copy-start(s32[128,8]{0,1:T(8,128)} %param.11) | copy-start | bytes 12292
  2.8 57.8 %copy-start.5 = (bf16[128,8]{0,1:T(8,128)(2,1)S(1)}, bf16[128,8]{0,1:T(8,128)(2,1)}, u32[]{:S(2)}) copy-start(bf16[128,8]{0,1:T(8,128)(2,1)} %param.12) | copy-start | bytes 6148
  56.3 78.4 %copy-start.2 = (bf16[4096,128]{1,0:T(8,128)(2,1)S(1)}, bf16[4096,128]{1,0:T(8,128)(2,1)}, u32[]{:S(2)}) copy-start(bf16[4096,128]{1,0:T(8,128)(2,1)} %cot_hbm.1) | copy-start | bytes 3145732
  56.3 33.6 %all-to-all-start.1 = ((bf16[32,13,4,128]{3,2,1,0:T(4,128)(2,1)}), bf16[32,13,4,128]{3,2,1,0:T(4,128)(2,1)S(1)}, u32[]{:S(2)}, u32[]{:S(2)}) async-start(bf16[32,13,4,128]{3,2,1,0:T(4,128)(2,1)} %bitcast.6), calls=%async_computation.1 | async-start | bytes 851968 | tf_op jit(solution)/shard_map/all_to_all | solution.py:186
  137.5 19.5 %all-to-all-start.2 = ((bf16[32,16,128]{2,1,0:T(8,128)(2,1)}), bf16[32,16,128]{2,1,0:T(8,128)(2,1)S(1)}, u32[]{:S(2)}, u32[]{:S(2)}) async-start(bf16[32,16,128]{2,1,0:T(8,128)(2,1)} %bitcast.8), calls=%async_computation.2 | async-start | bytes 262144 | tf_op jit(solution)/shard_map/all_to_all | solution.py:210

commit v6 on v5

--- a/solution.py
+++ b/solution.py
@@ -88,14 +88,14 @@
 
 def combine_kernel(w_ref, back_ref, out_ref, wide_ref):
     tok = w_ref.shape[0]
-    back = unpack(back_ref[...], wide_ref, out_ref.shape[2] // LANES)
+    back = unpack(back_ref[...], wide_ref, wide_ref.shape[0] // w_ref.shape[1])
     combined = jnp.dot(w_ref[...], back, preferred_element_type=F32).astype(BF16).astype(F32)
     largest = jnp.maximum(jnp.max(jnp.abs(combined), axis=1, keepdims=True), 2.0**-100)
     e = jnp.floor(jnp.log2(largest) + 1e-4) - 14.0
     whole = jnp.round(combined * power(-e).astype(F32))
     across = jnp.broadcast_to(e, (tok, tok)).T[:EXTRA]
-    across = jnp.concatenate([across] * (combined.shape[1] // tok), axis=1)
-    out_ref[0] = jnp.concatenate([whole, across]).astype(jnp.int32).astype(jnp.int16)
+    slabs = [whole[:, j : j + LANES] for j in range(0, whole.shape[1], LANES)]
+    out_ref[0] = jnp.concatenate(slabs + [across]).astype(jnp.int32).astype(jnp.int16)
 
 
 def part_copy(hbm, ref, sems, i):
@@ -106,9 +106,11 @@
 
 def rows_and_scales(coded_ref, n, tok):
     coded = coded_ref[n].astype(jnp.int32).astype(F32)
-    scale = power(coded[tok : tok + 1, :tok]).astype(F32)
+    end = coded.shape[0] - EXTRA
+    scale = power(coded[end : end + 1]).astype(F32)
     diagonal = jnp.where(iota((tok, tok), 0) == iota((tok, tok), 1), jnp.broadcast_to(scale, (tok, tok)), 0.0)
-    return coded[:tok].astype(BF16), diagonal.astype(BF16)
+    rows = jnp.concatenate([coded[j : j + tok] for j in range(0, end, tok)], axis=1)
+    return rows.astype(BF16), diagonal.astype(BF16)
 
 
 def grad_kernel(coded_ref, cot_hbm, out_ref, coded_hbm, cot_ref, coded_sem, cot_sems):
@@ -187,7 +189,7 @@
         produced.reshape(per_expert), "expert", split_axis=0, concat_axis=0, tiled=True
     ).reshape(packed.shape)
     coded = pl.pallas_call(
-        combine_kernel, out_shape=sds((1, tok + EXTRA, width), jnp.int16), in_specs=[VMEM] * 2, out_specs=VMEM,
+        combine_kernel, out_shape=sds((1, tok * width // LANES + EXTRA, LANES), jnp.int16), in_specs=[VMEM] * 2, out_specs=VMEM,
         scratch_shapes=[wide], compiler_params=vmem(8), name="combine",
     )(weight, back)
     gathered = lax.all_gather(coded, "expert", axis=0, tiled=True)

time: 172 us -> 171 us (level)
  no operation moved by 1% of the time
where the time goes in v6:
time: 171 us; the launch traced here: 170 us
  blocking collectives  107 us (63%)
  waiting for transfers between devices  33.8 us (20%)
  starting transfers between devices  13.9 us (8%)
  Pallas kernels  12.8 us (7%)
    all_to_all x1, blocking collectives, body(): lax.all_to_all(outgoing.reshape(per_expert), 'expert', split_axis=0, conc...  49.8 us
    all_gather x1, blocking collectives, body(): gathered = lax.all_gather(coded, 'expert', axis=0, tiled=True)  43.4 us
    all_to_all x1, waiting for transfers between devices, body(): lax.all_to_all(produced.reshape(per_expert), 'expert', split_axis=0, conc...  28.9 us
    all_to_all x1, blocking collectives, body(): lax.all_to_all(spread, 'dp', split_axis=0, concat_axis=0, tiled=True)  13.5 us
    all_to_all x1, starting transfers between devices, body(): lax.all_to_all(grad.reshape(n_dp, width // n_dp, cols), 'dp', split_axis=...  9.69 us
    pallas_call x1, Pallas kernels, body(): pl.pallas_call(mixed_kernel, out_shape=sds(cotangent.shape, BF16), in_spe...  4.92 us
    all_to_all x1, waiting for transfers between devices, body(): lax.all_to_all(grad.reshape(n_dp, width // n_dp, cols), 'dp', split_axis=...  4.9 us
    all_to_all x1, starting transfers between devices, body(): lax.all_to_all(produced.reshape(per_expert), 'expert', split_axis=0, conc...  4.25 us
  transfers between devices with their start and end apart: 2, of which 2 were waited for; matrix products, arithmetic and copies ran while one was open for 0% of the time, Pallas kernels for 3%

profile of v6, /device:TPU:1, one launch (start us, length us, event | category | flops | bytes accessed | tf_op | source)
XLA Modules:
  0.0 170.3 jit_solution(669404178607724620)
XLA Ops:
  0.6 0.0 copy-start.3
  0.6 0.7 copy-done.3
  1.3 0.0 copy-start.6
  1.3 0.9 copy-done.6
  2.2 0.0 copy-start
  2.2 0.0 copy-start.1
  2.2 0.6 dispatch.1
  2.8 0.0 copy-start.4
  2.8 0.0 copy-start.5
  2.8 49.8 %all_to_all.20 = bf16[32,13,4,128]{3,2,1,0:T(4,128)(2,1)S(1)} all-to-all(bf16[32,13,4,128]{3,2,1,0:T(4,128)(2,1)S(1)} %bitcast.16), channel_id=1, replica_groups=mesh['dp'=32,'expert'=32] {'expert'}, dimensions={0} | all-to-all | bytes 851968 | tf_op jit(solution)/shard_map/all_to_all | solution.py:181
  52.6 0.0 copy-done
  52.6 0.0 copy-done.1
  52.6 3.8 %expert.1 = bf16[1664,128]{1,0:T(8,128)(2,1)} custom-call(bf16[1664,128]{1,0:T(8,128)(2,1)S(1)} %bitcast.14, bf16[512,4096]{1,0:T(8,128)(2,1)S(1)} %bitcast.12, bf16[2048,512]{1,0:T(8,128)(2,1)S(1)} %bitcast.13), custom_call_target="tpu_custom_call" | custom-call | tf_op jit(solution)/shard_map/expert/pallas_call | solution.py:184
  56.3 0.0 copy-start.2
  56.3 4.2 %all-to-all-start.1 = ((bf16[32,13,4,128]{3,2,1,0:T(4,128)(2,1)}), bf16[32,13,4,128]{3,2,1,0:T(4,128)(2,1)S(1)}, u32[]{:S(2)}, u32[]{:S(2)}) async-start(bf16[32,13,4,128]{3,2,1,0:T(4,128)(2,1)} %bitcast.6), calls=%async_computation.1 | async-start | bytes 851968 | tf_op jit(solution)/shard_map/all_to_all | solution.py:188
  60.6 0.0 copy-done.4
  60.6 0.0 copy-done.5
  60.6 0.4 weight.1.w_ref
  61.0 28.9 %all-to-all-done.1 = bf16[32,13,4,128]{3,2,1,0:T(4,128)(2,1)S(1)} async-done(((bf16[32,13,4,128]{3,2,1,0:T(4,128)(2,1)}), bf16[32,13,4,128]{3,2,1,0:T(4,128)(2,1)S(1)}, u32[]{:S(2)}, u32[]{:S(2)}) %all-to-all-start.1) | async-done | bytes 426016 | tf_op jit(solution)/shard_map/all_to_all | solution.py:188
  89.9 0.4 combine.1
  90.3 43.4 %all-gather.1.coded_ref = s16[32,520,128]{2,1,0:T(8,128)(2,1)S(1)} all-gather(s16[1,520,128]{2,1,0:T(8,128)(2,1)S(1)} %combine.1), channel_id=1, replica_groups=mesh['dp'=32,'expert'=32] {'expert'}, dimensions={0}, use_global_device_ids=true | all-gather | bytes 4392960 | tf_op jit(solution)/shard_map/all_gather | solution.py:195
  133.7 0.0 copy-done.2
  133.7 2.7 %grad.1 = (bf16[512,128]{1,0:T(8,128)(2,1)}, s16[64,520,128]{2,1,0:T(8,128)(2,1)}) custom-call(s16[32,520,128]{2,1,0:T(8,128)(2,1)S(1)} %all-gather.1.coded_ref, bf16[4096,128]{1,0:T(8,128)(2,1)S(1)} %copy-done.2), custom_call_target="tpu_custom_call" | custom-call | tf_op jit(solution)/shard_map/grad/pallas_call | solution.py:201
  136.5 9.7 %all-to-all-start.2 = ((bf16[32,16,128]{2,1,0:T(8,128)(2,1)}), bf16[32,16,128]{2,1,0:T(8,128)(2,1)S(1)}, u32[]{:S(2)}, u32[]{:S(2)}) async-start(bf16[32,16,128]{2,1,0:T(8,128)(2,1)} %bitcast.8), calls=%async_computation.2 | async-start | bytes 262144 | tf_op jit(solution)/shard_map/all_to_all | solution.py:212
  146.2 4.9 %mixed.1 = bf16[4096,128]{1,0:T(8,128)(2,1)} custom-call(s16[64,520,128]{2,1,0:T(8,128)(2,1)} %get-tuple-element.7.coded_hbm, bf16[512,128]{1,0:T(8,128)(2,1)} %up_ref.1), custom_call_target="tpu_custom_call" | custom-call | flops 536870912 | bytes 6291456 | tf_op jit(solution)/shard_map/mixed/pallas_call | solution.py:206
  151.1 4.9 %all-to-all-done.2 = bf16[32,16,128]{2,1,0:T(8,128)(2,1)S(1)} async-done(((bf16[32,16,128]{2,1,0:T(8,128)(2,1)}), bf16[32,16,128]{2,1,0:T(8,128)(2,1)S(1)}, u32[]{:S(2)}, u32[]{:S(2)}) %all-to-all-start.2) | async-done | bytes 131104 | tf_op jit(solution)/shard_map/all_to_all | solution.py:212
  156.0 13.5 %all_to_all.21 = bf16[32,16,128]{2,1,0:T(8,128)(2,1)S(1)} all-to-all(bf16[32,16,128]{2,1,0:T(8,128)(2,1)S(1)} %broadcast_in_dim.2), channel_id=1, replica_groups=mesh['dp'=32,'expert'=32] {'dp'}, dimensions={0} | all-to-all | bytes 262144 | tf_op jit(solution)/shard_map/all_to_all | solution.py:216
  169.5 0.7 bitcast_convert_fusion
  (2 shorter events, 0.1 us)
Async XLA Ops:
  0.6 0.7 copy-start.3
  1.3 0.9 copy-start.6
  2.2 50.3 %copy-start = (bf16[1,512,4096]{2,1,0:T(8,128)(2,1)S(1)}, bf16[1,512,4096]{2,1,0:T(8,128)(2,1)}, u32[]{:S(2)}) copy-start(bf16[1,512,4096]{2,1,0:T(8,128)(2,1)} %param.9) | copy-start | bytes 12582916
  2.2 50.3 %copy-start.1 = (bf16[1,2048,512]{2,1,0:T(8,128)(2,1)S(1)}, bf16[1,2048,512]{2,1,0:T(8,128)(2,1)}, u32[]{:S(2)}) copy-start(bf16[1,2048,512]{2,1,0:T(8,128)(2,1)} %param.10) | copy-start | bytes 6291460
  2.8 57.8 %copy-start.4 = (s32[128,8]{0,1:T(8,128)S(1)}, s32[128,8]{0,1:T(8,128)}, u32[]{:S(2)}) copy-start(s32[128,8]{0,1:T(8,128)} %param.11) | copy-start | bytes 12292
  2.8 57.8 %copy-start.5 = (bf16[128,8]{0,1:T(8,128)(2,1)S(1)}, bf16[128,8]{0,1:T(8,128)(2,1)}, u32[]{:S(2)}) copy-start(bf16[128,8]{0,1:T(8,128)(2,1)} %param.12) | copy-start | bytes 6148
  56.3 77.4 %copy-start.2 = (bf16[4096,128]{1,0:T(8,128)(2,1)S(1)}, bf16[4096,128]{1,0:T(8,128)(2,1)}, u32[]{:S(2)}) copy-start(bf16[4096,128]{1,0:T(8,128)(2,1)} %cot_hbm.1) | copy-start | bytes 3145732
  56.3 33.6 %all-to-all-start.1 = ((bf16[32,13,4,128]{3,2,1,0:T(4,128)(2,1)}), bf16[32,13,4,128]{3,2,1,0:T(4,128)(2,1)S(1)}, u32[]{:S(2)}, u32[]{:S(2)}) async-start(bf16[32,13,4,128]{3,2,1,0:T(4,128)(2,1)} %bitcast.6), calls=%async_computation.1 | async-start | bytes 851968 | tf_op jit(solution)/shard_map/all_to_all | solution.py:188
  136.5 19.5 %all-to-all-start.2 = ((bf16[32,16,128]{2,1,0:T(8,128)(2,1)}), bf16[32,16,128]{2,1,0:T(8,128)(2,1)S(1)}, u32[]{:S(2)}, u32[]{:S(2)}) async-start(bf16[32,16,128]{2,1,0:T(8,128)(2,1)} %bitcast.8), calls=%async_computation.2 | async-start | bytes 262144 | tf_op jit(solution)/shard_map/all_to_all | solution.py:212

commit v7 on v6

--- a/solution.py
+++ b/solution.py
@@ -113,17 +113,14 @@
     return rows.astype(BF16), diagonal.astype(BF16)
 
 
-def grad_kernel(coded_ref, cot_hbm, out_ref, coded_hbm, cot_ref, coded_sem, cot_sems):
-    sources, parts = coded_ref.shape[0], cot_sems.shape[0]
+def grad_kernel(coded_ref, cot_ref, out_ref, coded_hbm, coded_sem):
+    sources = coded_ref.shape[0]
     tok = cot_ref.shape[0] // sources
-    many = sources // parts
-    for i in range(parts):
-        part_copy(cot_hbm, cot_ref, cot_sems, i).start()
+    many = 8
     keep = pltpu.make_async_copy(coded_ref, coded_hbm.at[pl.ds(0, sources)], coded_sem)
     keep.start()
     total = None
-    for i in range(parts):
-        part_copy(cot_hbm, cot_ref, cot_sems, i).wait()
+    for i in range(sources // many):
         rows, cots = [], []
         for n in range(i * many, (i + 1) * many):
             coded, diagonal = rows_and_scales(coded_ref, n, tok)
@@ -154,6 +151,11 @@
         part_copy(out_ref, out_hbm, out_sems, i).start()
     for i in range(parts):
         part_copy(out_ref, out_hbm, out_sems, i).wait()
+
+
+def sum_kernel(parts_ref, out_ref):
+    total = jnp.sum(parts_ref[...].astype(F32), axis=0).astype(BF16)
+    out_ref[...] = jnp.broadcast_to(total[None], out_ref.shape)
 
 
 def body(latent, up_proj, expert_in, expert_out, routes, gates, cotangent):
@@ -200,8 +202,8 @@
     room = sds((2 * n_expert,) + gathered.shape[1:], gathered.dtype)
     grad, kept = pl.pallas_call(
         grad_kernel, out_shape=[sds((width, cols), BF16), room],
-        in_specs=[VMEM, HBM], out_specs=[VMEM, HBM],
-        scratch_shapes=whole + [pltpu.SemaphoreType.DMA, sems[0]], compiler_params=vmem(47), name="grad",
+        in_specs=[VMEM] * 2, out_specs=[VMEM, HBM],
+        scratch_shapes=[pltpu.SemaphoreType.DMA], compiler_params=vmem(47), name="grad",
     )(gathered, cotangent)
     mixed = pl.pallas_call(
         mixed_kernel, out_shape=sds(cotangent.shape, BF16), in_specs=[HBM, VMEM], out_specs=HBM,
@@ -211,8 +213,10 @@
 
     parts = lax.all_to_all(grad.reshape(n_dp, width // n_dp, cols), "dp", split_axis=0, concat_axis=0, tiled=True)
     parts, mixed = lax.optimization_barrier((parts, mixed))
-    mine = jnp.sum(parts.astype(F32), axis=0).astype(BF16)
-    spread = jnp.broadcast_to(mine[None], (n_dp,) + mine.shape)
+    spread = pl.pallas_call(
+        sum_kernel, out_shape=sds(parts.shape, BF16), in_specs=[VMEM], out_specs=VMEM,
+        compiler_params=vmem(8), name="sum",
+    )(parts)
     grad_up = lax.all_to_all(spread, "dp", split_axis=0, concat_axis=0, tiled=True).astype(F32)
     return mixed, grad_up.reshape(width, cols)
 

time: 171 us -> 171 us (level)
  no operation moved by 1% of the time
where the time goes in v7:
time: 171 us; the launch traced here: 170 us
  blocking collectives  107 us (63%)
  waiting for transfers between devices  33.7 us (20%)
  starting transfers between devices  13.9 us (8%)
  Pallas kernels  12.9 us (8%)
    all_to_all x1, blocking collectives, body(): lax.all_to_all(outgoing.reshape(per_expert), 'expert', split_axis=0, conc...  49.8 us
    all_gather x1, blocking collectives, body(): gathered = lax.all_gather(coded, 'expert', axis=0, tiled=True)  43.4 us
    all_to_all x1, waiting for transfers between devices, body(): lax.all_to_all(produced.reshape(per_expert), 'expert', split_axis=0, conc...  28.9 us
    all_to_all x1, blocking collectives, body(): lax.all_to_all(spread, 'dp', split_axis=0, concat_axis=0, tiled=True)  13.5 us
    all_to_all x1, starting transfers between devices, body(): lax.all_to_all(grad.reshape(n_dp, width // n_dp, cols), 'dp', split_axis=...  9.69 us
    pallas_call x1, Pallas kernels, body(): pl.pallas_call(mixed_kernel, out_shape=sds(cotangent.shape, BF16), in_spe...  4.91 us
    all_to_all x1, waiting for transfers between devices, body(): lax.all_to_all(grad.reshape(n_dp, width // n_dp, cols), 'dp', split_axis=...  4.89 us
    all_to_all x1, starting transfers between devices, body(): lax.all_to_all(produced.reshape(per_expert), 'expert', split_axis=0, conc...  4.25 us
  transfers between devices with their start and end apart: 2, of which 2 were waited for; matrix products, arithmetic and copies ran while one was open for 0% of the time, Pallas kernels for 3%

profile of v7, /device:TPU:1, one launch (start us, length us, event | category | flops | bytes accessed | tf_op | source)
XLA Modules:
  0.0 170.3 jit_solution(13933948572515760838)
XLA Ops:
  0.6 0.0 copy-start.3
  0.6 0.7 copy-done.3
  1.3 0.0 copy-start.6
  1.3 0.9 copy-done.6
  2.2 0.0 copy-start
  2.2 0.0 copy-start.1
  2.2 0.6 dispatch.1
  2.8 0.0 copy-start.4
  2.8 0.0 copy-start.5
  2.8 49.8 %all_to_all.20 = bf16[32,13,4,128]{3,2,1,0:T(4,128)(2,1)S(1)} all-to-all(bf16[32,13,4,128]{3,2,1,0:T(4,128)(2,1)S(1)} %bitcast.16), channel_id=1, replica_groups=mesh['dp'=32,'expert'=32] {'expert'}, dimensions={0} | all-to-all | bytes 851968 | tf_op jit(solution)/shard_map/all_to_all | solution.py:183
  52.6 0.0 copy-done
  52.6 0.0 copy-done.1
  52.6 3.8 %expert.1 = bf16[1664,128]{1,0:T(8,128)(2,1)} custom-call(bf16[1664,128]{1,0:T(8,128)(2,1)S(1)} %bitcast.14, bf16[512,4096]{1,0:T(8,128)(2,1)S(1)} %bitcast.12, bf16[2048,512]{1,0:T(8,128)(2,1)S(1)} %bitcast.13), custom_call_target="tpu_custom_call" | custom-call | tf_op jit(solution)/shard_map/expert/pallas_call | solution.py:186
  56.3 0.0 copy-start.2
  56.3 4.2 %all-to-all-start.1 = ((bf16[32,13,4,128]{3,2,1,0:T(4,128)(2,1)}), bf16[32,13,4,128]{3,2,1,0:T(4,128)(2,1)S(1)}, u32[]{:S(2)}, u32[]{:S(2)}) async-start(bf16[32,13,4,128]{3,2,1,0:T(4,128)(2,1)} %bitcast.6), calls=%async_computation.1 | async-start | bytes 851968 | tf_op jit(solution)/shard_map/all_to_all | solution.py:190
  60.6 0.0 copy-done.4
  60.6 0.0 copy-done.5
  60.6 0.4 weight.1.w_ref
  61.0 28.9 %all-to-all-done.1 = bf16[32,13,4,128]{3,2,1,0:T(4,128)(2,1)S(1)} async-done(((bf16[32,13,4,128]{3,2,1,0:T(4,128)(2,1)}), bf16[32,13,4,128]{3,2,1,0:T(4,128)(2,1)S(1)}, u32[]{:S(2)}, u32[]{:S(2)}) %all-to-all-start.1) | async-done | bytes 426016 | tf_op jit(solution)/shard_map/all_to_all | solution.py:190
  89.9 0.4 combine.1
  90.3 43.4 %all-gather.1.coded_ref = s16[32,520,128]{2,1,0:T(8,128)(2,1)S(1)} all-gather(s16[1,520,128]{2,1,0:T(8,128)(2,1)S(1)} %combine.1), channel_id=1, replica_groups=mesh['dp'=32,'expert'=32] {'expert'}, dimensions={0}, use_global_device_ids=true | all-gather | bytes 4392960 | tf_op jit(solution)/shard_map/all_gather | solution.py:197
  133.7 0.0 copy-done.2
  133.7 2.8 %grad.1 = (bf16[512,128]{1,0:T(8,128)(2,1)}, s16[64,520,128]{2,1,0:T(8,128)(2,1)}) custom-call(s16[32,520,128]{2,1,0:T(8,128)(2,1)S(1)} %all-gather.1.coded_ref, bf16[4096,128]{1,0:T(8,128)(2,1)S(1)} %copy-done.2), custom_call_target="tpu_custom_call" | custom-call | tf_op jit(solution)/shard_map/grad/pallas_call | solution.py:203
  136.5 9.7 %all-to-all-start.2 = ((bf16[32,16,128]{2,1,0:T(8,128)(2,1)}), bf16[32,16,128]{2,1,0:T(8,128)(2,1)S(1)}, u32[]{:S(2)}, u32[]{:S(2)}) async-start(bf16[32,16,128]{2,1,0:T(8,128)(2,1)} %bitcast.8), calls=%async_computation.2 | async-start | bytes 262144 | tf_op jit(solution)/shard_map/all_to_all | solution.py:214
  146.2 4.9 %mixed.1 = bf16[4096,128]{1,0:T(8,128)(2,1)} custom-call(s16[64,520,128]{2,1,0:T(8,128)(2,1)} %get-tuple-element.7.coded_hbm, bf16[512,128]{1,0:T(8,128)(2,1)} %up_ref.1), custom_call_target="tpu_custom_call" | custom-call | flops 536870912 | bytes 6291456 | tf_op jit(solution)/shard_map/mixed/pallas_call | solution.py:208
  151.1 4.9 %all-to-all-done.2.parts_ref = bf16[32,16,128]{2,1,0:T(8,128)(2,1)S(1)} async-done(((bf16[32,16,128]{2,1,0:T(8,128)(2,1)}), bf16[32,16,128]{2,1,0:T(8,128)(2,1)S(1)}, u32[]{:S(2)}, u32[]{:S(2)}) %all-to-all-start.2) | async-done | bytes 131104 | tf_op jit(solution)/shard_map/all_to_all | solution.py:214
  156.1 13.5 %all_to_all.21 = bf16[32,16,128]{2,1,0:T(8,128)(2,1)S(1)} all-to-all(bf16[32,16,128]{2,1,0:T(8,128)(2,1)S(1)} %sum.1), channel_id=1, replica_groups=mesh['dp'=32,'expert'=32] {'dp'}, dimensions={0} | all-to-all | bytes 262144 | tf_op jit(solution)/shard_map/all_to_all | solution.py:220
  169.5 0.7 bitcast_convert_fusion
  (1 shorter events, 0.0 us)
Async XLA Ops:
  0.6 0.7 copy-start.3
  1.3 0.9 copy-start.6
  2.2 50.3 %copy-start = (bf16[1,512,4096]{2,1,0:T(8,128)(2,1)S(1)}, bf16[1,512,4096]{2,1,0:T(8,128)(2,1)}, u32[]{:S(2)}) copy-start(bf16[1,512,4096]{2,1,0:T(8,128)(2,1)} %param.9) | copy-start | bytes 12582916
  2.2 50.3 %copy-start.1 = (bf16[1,2048,512]{2,1,0:T(8,128)(2,1)S(1)}, bf16[1,2048,512]{2,1,0:T(8,128)(2,1)}, u32[]{:S(2)}) copy-start(bf16[1,2048,512]{2,1,0:T(8,128)(2,1)} %param.10) | copy-start | bytes 6291460
  2.8 57.8 %copy-start.4 = (s32[128,8]{0,1:T(8,128)S(1)}, s32[128,8]{0,1:T(8,128)}, u32[]{:S(2)}) copy-start(s32[128,8]{0,1:T(8,128)} %param.11) | copy-start | bytes 12292
  2.8 57.8 %copy-start.5 = (bf16[128,8]{0,1:T(8,128)(2,1)S(1)}, bf16[128,8]{0,1:T(8,128)(2,1)}, u32[]{:S(2)}) copy-start(bf16[128,8]{0,1:T(8,128)(2,1)} %param.12) | copy-start | bytes 6148
  56.3 77.4 %copy-start.2 = (bf16[4096,128]{1,0:T(8,128)(2,1)S(1)}, bf16[4096,128]{1,0:T(8,128)(2,1)}, u32[]{:S(2)}) copy-start(bf16[4096,128]{1,0:T(8,128)(2,1)} %cot_ref.1) | copy-start | bytes 3145732
  56.3 33.6 %all-to-all-start.1 = ((bf16[32,13,4,128]{3,2,1,0:T(4,128)(2,1)}), bf16[32,13,4,128]{3,2,1,0:T(4,128)(2,1)S(1)}, u32[]{:S(2)}, u32[]{:S(2)}) async-start(bf16[32,13,4,128]{3,2,1,0:T(4,128)(2,1)} %bitcast.6), calls=%async_computation.1 | async-start | bytes 851968 | tf_op jit(solution)/shard_map/all_to_all | solution.py:190
  136.5 19.5 %all-to-all-start.2 = ((bf16[32,16,128]{2,1,0:T(8,128)(2,1)}), bf16[32,16,128]{2,1,0:T(8,128)(2,1)S(1)}, u32[]{:S(2)}, u32[]{:S(2)}) async-start(bf16[32,16,128]{2,1,0:T(8,128)(2,1)} %bitcast.8), calls=%async_computation.2 | async-start | bytes 262144 | tf_op jit(solution)/shard_map/all_to_all | solution.py:214

commit v8 on v7

--- a/solution.py
+++ b/solution.py
@@ -1,3 +1,5 @@
+import functools
+
 import jax
 import jax.numpy as jnp
 from jax import lax
@@ -134,14 +136,15 @@
     keep.wait()
 
 
-def mixed_kernel(coded_hbm, up_ref, out_hbm, coded_ref, out_ref, coded_sems, out_sems):
+def mixed_kernel(mine, coded_hbm, up_ref, *rest):
+    out_hbm, coded_ref, out_ref, coded_sems, out_sems = rest[-5:]
     sources, parts = coded_ref.shape[0], coded_sems.shape[0]
     tok = out_ref.shape[0] // sources
     many = sources // parts
     ones = jnp.ones((tok, out_ref.shape[1]), BF16)
-    for i in range(parts):
+    for i in mine:
         part_copy(coded_hbm, coded_ref, coded_sems, i).start()
-    for i in range(parts):
+    for i in mine:
         part_copy(coded_hbm, coded_ref, coded_sems, i).wait()
         for n in range(i * many, (i + 1) * many):
             coded, diagonal = rows_and_scales(coded_ref, n, tok)
@@ -149,7 +152,7 @@
             mixed = jnp.dot(coded, up_ref[...], preferred_element_type=F32) * scale
             out_ref[n * tok : (n + 1) * tok, :] = mixed.astype(BF16)
         part_copy(out_ref, out_hbm, out_sems, i).start()
-    for i in range(parts):
+    for i in mine:
         part_copy(out_ref, out_hbm, out_sems, i).wait()
 
 
@@ -205,18 +208,27 @@
         in_specs=[VMEM] * 2, out_specs=[VMEM, HBM],
         scratch_shapes=[pltpu.SemaphoreType.DMA], compiler_params=vmem(47), name="grad",
     )(gathered, cotangent)
-    mixed = pl.pallas_call(
-        mixed_kernel, out_shape=sds(cotangent.shape, BF16), in_specs=[HBM, VMEM], out_specs=HBM,
-        scratch_shapes=coded_parts + whole + sems, compiler_params=vmem(60), name="mixed",
-        cost_estimate=pl.CostEstimate(flops=2 * cotangent.shape[0] * width * cols, bytes_accessed=6 << 20, transcendentals=0),
-    )(kept, up_proj)
-
-    parts = lax.all_to_all(grad.reshape(n_dp, width // n_dp, cols), "dp", split_axis=0, concat_axis=0, tiled=True)
-    parts, mixed = lax.optimization_barrier((parts, mixed))
+    def project(mine, kept, *before):
+        return pl.pallas_call(
+            functools.partial(mixed_kernel, mine), out_shape=sds(cotangent.shape, BF16),
+            in_specs=[HBM, VMEM] + [HBM] * len(before), out_specs=HBM,
+            scratch_shapes=coded_parts + whole + sems, compiler_params=vmem(60), name=f"mixed{mine[0]}",
+            input_output_aliases={2: 0} if before else {},
+            cost_estimate=pl.CostEstimate(
+                flops=cotangent.shape[0] * width * cols, bytes_accessed=3 << 20, transcendentals=0
+            ),
+        )(kept, up_proj, *before)
+
+    mixed = project(range(parts // 2), kept)
+
+    summands = lax.all_to_all(grad.reshape(n_dp, width // n_dp, cols), "dp", split_axis=0, concat_axis=0, tiled=True)
+    summands, mixed = lax.optimization_barrier((summands, mixed))
     spread = pl.pallas_call(
-        sum_kernel, out_shape=sds(parts.shape, BF16), in_specs=[VMEM], out_specs=VMEM,
+        sum_kernel, out_shape=sds(summands.shape, BF16), in_specs=[VMEM], out_specs=VMEM,
         compiler_params=vmem(8), name="sum",
-    )(parts)
+    )(summands)
+    spread, kept = lax.optimization_barrier((spread, kept))
+    mixed = project(range(parts // 2, parts), kept, mixed)
     grad_up = lax.all_to_all(spread, "dp", split_axis=0, concat_axis=0, tiled=True).astype(F32)
     return mixed, grad_up.reshape(width, cols)
 

time: 171 us -> 172 us (level)
  blocking collectives: 107 us -> 93.1 us
  waiting for transfers between devices: 33.7 us -> 40.3 us
  starting transfers between devices: 13.9 us -> 17.8 us
  Pallas kernels: 12.9 us -> 16.5 us
    all_to_all x1 -> x0, blocking collectives: 13.5 us -> none  [body(): lax.all_to_all(spread, 'dp', split_axis=0, concat_axis=0, tiled=True)]
    all_to_all x0 -> x1, waiting for transfers between devices: none -> 5.5 us  [body(): lax.all_to_all(spread, 'dp', split_axis=0, concat_axis=0, tiled=True)]
    all_to_all x0 -> x1, starting transfers between devices: none -> 3.86 us  [body(): lax.all_to_all(spread, 'dp', split_axis=0, concat_axis=0, tiled=True)]
    pallas_call x2 -> x3, Pallas kernels: 4.96 us -> 8.51 us  [the longest x2 7.81 us: project(): pl.pallas_call(functools.partial(mixed_kernel, mine), out_shape=sds(cotan...]
  transfers between devices with their start and end apart: 2 -> 3, of which waited for: 2 -> 3; matrix products, arithmetic and copies ran while one was open for 0% -> 0% of each run, Pallas kernels for 3% -> 5%
where the time goes in v8:
time: 172 us; the launch traced here: 171 us
  blocking collectives  93.1 us (54%)
  waiting for transfers between devices  40.3 us (23%)
  starting transfers between devices  17.8 us (10%)
  Pallas kernels  16.5 us (10%)
    all_to_all x1, blocking collectives, body(): lax.all_to_all(outgoing.reshape(per_expert), 'expert', split_axis=0, conc...  49.8 us
    all_gather x1, blocking collectives, body(): gathered = lax.all_gather(coded, 'expert', axis=0, tiled=True)  43.4 us
    all_to_all x1, waiting for transfers between devices, body(): lax.all_to_all(produced.reshape(per_expert), 'expert', split_axis=0, conc...  28.9 us
    all_to_all x1, starting transfers between devices, body(): lax.all_to_all(grad.reshape(n_dp, width // n_dp, cols), 'dp', split_axis=...  9.69 us
    pallas_call x2, Pallas kernels, project(): pl.pallas_call(functools.partial(mixed_kernel, mine), out_shape=sds(cotan...  7.81 us
    all_to_all x1, waiting for transfers between devices, body(): lax.all_to_all(grad.reshape(n_dp, width // n_dp, cols), 'dp', split_axis=...  5.9 us
    all_to_all x1, waiting for transfers between devices, body(): lax.all_to_all(spread, 'dp', split_axis=0, concat_axis=0, tiled=True)  5.5 us
    all_to_all x1, starting transfers between devices, body(): lax.all_to_all(produced.reshape(per_expert), 'expert', split_axis=0, conc...  4.25 us
  transfers between devices with their start and end apart: 3, of which 3 were waited for; matrix products, arithmetic and copies ran while one was open for 0% of the time, Pallas kernels for 5%

profile of v8, /device:TPU:1, one launch (start us, length us, event | category | flops | bytes accessed | tf_op | source)
XLA Modules:
  0.0 170.7 jit_solution(4847732130616312111)
XLA Ops:
  0.6 0.0 copy-start.3
  0.6 0.7 copy-done.3
  1.3 0.0 copy-start.6
  1.3 0.9 copy-done.6
  2.2 0.0 copy-start
  2.2 0.0 copy-start.1
  2.2 0.6 dispatch.1
  2.8 0.0 copy-start.4
  2.8 0.0 copy-start.5
  2.8 49.8 %all_to_all.20 = bf16[32,13,4,128]{3,2,1,0:T(4,128)(2,1)S(1)} all-to-all(bf16[32,13,4,128]{3,2,1,0:T(4,128)(2,1)S(1)} %bitcast.16), channel_id=1, replica_groups=mesh['dp'=32,'expert'=32] {'expert'}, dimensions={0} | all-to-all | bytes 851968 | tf_op jit(solution)/shard_map/all_to_all | solution.py:186
  52.6 0.0 copy-done
  52.6 0.0 copy-done.1
  52.6 3.8 %expert.1 = bf16[1664,128]{1,0:T(8,128)(2,1)} custom-call(bf16[1664,128]{1,0:T(8,128)(2,1)S(1)} %bitcast.14, bf16[512,4096]{1,0:T(8,128)(2,1)S(1)} %bitcast.12, bf16[2048,512]{1,0:T(8,128)(2,1)S(1)} %bitcast.13), custom_call_target="tpu_custom_call" | custom-call | tf_op jit(solution)/shard_map/expert/pallas_call | solution.py:189
  56.3 0.0 copy-start.2
  56.3 4.2 %all-to-all-start.1 = ((bf16[32,13,4,128]{3,2,1,0:T(4,128)(2,1)}), bf16[32,13,4,128]{3,2,1,0:T(4,128)(2,1)S(1)}, u32[]{:S(2)}, u32[]{:S(2)}) async-start(bf16[32,13,4,128]{3,2,1,0:T(4,128)(2,1)} %bitcast.6), calls=%async_computation.1 | async-start | bytes 851968 | tf_op jit(solution)/shard_map/all_to_all | solution.py:193
  60.6 0.0 copy-done.4
  60.6 0.0 copy-done.5
  60.6 0.4 weight.1.w_ref
  61.0 28.9 %all-to-all-done.1 = bf16[32,13,4,128]{3,2,1,0:T(4,128)(2,1)S(1)} async-done(((bf16[32,13,4,128]{3,2,1,0:T(4,128)(2,1)}), bf16[32,13,4,128]{3,2,1,0:T(4,128)(2,1)S(1)}, u32[]{:S(2)}, u32[]{:S(2)}) %all-to-all-start.1) | async-done | bytes 426016 | tf_op jit(solution)/shard_map/all_to_all | solution.py:193
  89.9 0.4 combine.1
  90.3 43.4 %all-gather.1.coded_ref = s16[32,520,128]{2,1,0:T(8,128)(2,1)S(1)} all-gather(s16[1,520,128]{2,1,0:T(8,128)(2,1)S(1)} %combine.1), channel_id=1, replica_groups=mesh['dp'=32,'expert'=32] {'expert'}, dimensions={0}, use_global_device_ids=true | all-gather | bytes 4392960 | tf_op jit(solution)/shard_map/all_gather | solution.py:200
  133.7 0.0 copy-done.2
  133.7 2.8 %grad.1 = (bf16[512,128]{1,0:T(8,128)(2,1)}, s16[64,520,128]{2,1,0:T(8,128)(2,1)}) custom-call(s16[32,520,128]{2,1,0:T(8,128)(2,1)S(1)} %all-gather.1.coded_ref, bf16[4096,128]{1,0:T(8,128)(2,1)S(1)} %copy-done.2), custom_call_target="tpu_custom_call" | custom-call | tf_op jit(solution)/shard_map/grad/pallas_call | solution.py:206
  136.5 9.7 %all-to-all-start.2 = ((bf16[32,16,128]{2,1,0:T(8,128)(2,1)}), bf16[32,16,128]{2,1,0:T(8,128)(2,1)S(1)}, u32[]{:S(2)}, u32[]{:S(2)}) async-start(bf16[32,16,128]{2,1,0:T(8,128)(2,1)} %bitcast.8), calls=%async_computation.2 | async-start | bytes 262144 | tf_op jit(solution)/shard_map/all_to_all | solution.py:224
  146.2 3.9 %mixed0.1.rest_0_ = bf16[4096,128]{1,0:T(8,128)(2,1)} custom-call(s16[64,520,128]{2,1,0:T(8,128)(2,1)} %get-tuple-element.11.coded_hbm, bf16[512,128]{1,0:T(8,128)(2,1)} %up_ref.3), custom_call_target="tpu_custom_call" | custom-call | flops 268435456 | bytes 3145728 | tf_op jit(solution)/shard_map/mixed0/pallas_call | solution.py:212
  150.1 5.9 %all-to-all-done.2.parts_ref = bf16[32,16,128]{2,1,0:T(8,128)(2,1)S(1)} async-done(((bf16[32,16,128]{2,1,0:T(8,128)(2,1)}), bf16[32,16,128]{2,1,0:T(8,128)(2,1)S(1)}, u32[]{:S(2)}, u32[]{:S(2)}) %all-to-all-start.2) | async-done | bytes 131104 | tf_op jit(solution)/shard_map/all_to_all | solution.py:224
  156.0 0.7 sum.1
  156.7 3.9 %all-to-all-start.3 = ((bf16[32,16,128]{2,1,0:T(8,128)(2,1)}), bf16[32,16,128]{2,1,0:T(8,128)(2,1)S(1)}, u32[]{:S(2)}, u32[]{:S(2)}) async-start(bf16[32,16,128]{2,1,0:T(8,128)(2,1)} %sum.1), calls=%async_computation.3 | async-start | bytes 262144 | tf_op jit(solution)/shard_map/all_to_all | solution.py:232
  160.6 3.9 %mixed2.1 = bf16[4096,128]{1,0:T(8,128)(2,1)} custom-call(s16[64,520,128]{2,1,0:T(8,128)(2,1)} %get-tuple-element.11.coded_hbm, bf16[512,128]{1,0:T(8,128)(2,1)} %up_ref.3, bf16[4096,128]{1,0:T(8,128)(2,1)} %mixed0.1.rest_0_), custom_call_target="tpu_custom_call", output_to_operand_aliasing={{}: (2, {})} | custom-call | flops 268435456 | bytes 3145728 | tf_op jit(solution)/shard_map/mixed2/pallas_call | solution.py:212
  164.5 5.5 %all-to-all-done.3 = bf16[32,16,128]{2,1,0:T(8,128)(2,1)S(1)} async-done(((bf16[32,16,128]{2,1,0:T(8,128)(2,1)}), bf16[32,16,128]{2,1,0:T(8,128)(2,1)S(1)}, u32[]{:S(2)}, u32[]{:S(2)}) %all-to-all-start.3) | async-done | bytes 131104 | tf_op jit(solution)/shard_map/all_to_all | solution.py:232
  170.0 0.7 bitcast_convert_fusion
Async XLA Ops:
  0.6 0.7 copy-start.3
  1.3 0.9 copy-start.6
  2.2 50.3 %copy-start = (bf16[1,512,4096]{2,1,0:T(8,128)(2,1)S(1)}, bf16[1,512,4096]{2,1,0:T(8,128)(2,1)}, u32[]{:S(2)}) copy-start(bf16[1,512,4096]{2,1,0:T(8,128)(2,1)} %param.9) | copy-start | bytes 12582916
  2.2 50.3 %copy-start.1 = (bf16[1,2048,512]{2,1,0:T(8,128)(2,1)S(1)}, bf16[1,2048,512]{2,1,0:T(8,128)(2,1)}, u32[]{:S(2)}) copy-start(bf16[1,2048,512]{2,1,0:T(8,128)(2,1)} %param.10) | copy-start | bytes 6291460
  2.8 57.8 %copy-start.4 = (s32[128,8]{0,1:T(8,128)S(1)}, s32[128,8]{0,1:T(8,128)}, u32[]{:S(2)}) copy-start(s32[128,8]{0,1:T(8,128)} %param.11) | copy-start | bytes 12292
  2.8 57.8 %copy-start.5 = (bf16[128,8]{0,1:T(8,128)(2,1)S(1)}, bf16[128,8]{0,1:T(8,128)(2,1)}, u32[]{:S(2)}) copy-start(bf16[128,8]{0,1:T(8,128)(2,1)} %param.12) | copy-start | bytes 6148
  56.3 77.4 %copy-start.2 = (bf16[4096,128]{1,0:T(8,128)(2,1)S(1)}, bf16[4096,128]{1,0:T(8,128)(2,1)}, u32[]{:S(2)}) copy-start(bf16[4096,128]{1,0:T(8,128)(2,1)} %cot_ref.1) | copy-start | bytes 3145732
  56.3 33.6 %all-to-all-start.1 = ((bf16[32,13,4,128]{3,2,1,0:T(4,128)(2,1)}), bf16[32,13,4,128]{3,2,1,0:T(4,128)(2,1)S(1)}, u32[]{:S(2)}, u32[]{:S(2)}) async-start(bf16[32,13,4,128]{3,2,1,0:T(4,128)(2,1)} %bitcast.6), calls=%async_computation.1 | async-start | bytes 851968 | tf_op jit(solution)/shard_map/all_to_all | solution.py:193
  136.5 19.5 %all-to-all-start.2 = ((bf16[32,16,128]{2,1,0:T(8,128)(2,1)}), bf16[32,16,128]{2,1,0:T(8,128)(2,1)S(1)}, u32[]{:S(2)}, u32[]{:S(2)}) async-start(bf16[32,16,128]{2,1,0:T(8,128)(2,1)} %bitcast.8), calls=%async_computation.2 | async-start | bytes 262144 | tf_op jit(solution)/shard_map/all_to_all | solution.py:224
  156.7 13.3 %all-to-all-start.3 = ((bf16[32,16,128]{2,1,0:T(8,128)(2,1)}), bf16[32,16,128]{2,1,0:T(8,128)(2,1)S(1)}, u32[]{:S(2)}, u32[]{:S(2)}) async-start(bf16[32,16,128]{2,1,0:T(8,128)(2,1)} %sum.1), calls=%async_computation.3 | async-start | bytes 262144 | tf_op jit(solution)/shard_map/all_to_all | solution.py:232
